TPU v7x, 128 devices: a whole 4x4x4 slice. The times are simulated.
128 devices in a mesh: head: 4 (over y_lo, core), inner: 8 (over y_hi, x), outer: 4 (over z).
Axes of the slice: x: 4, y: 4 (y_hi: 2, y_lo: 2; y = y_hi * 2 + y_lo), z: 4, core: 2. Of those that a mesh axis runs over, the one named last changes fastest.
Arguments:
- queries: bfloat16 [8192, 4096], P(('head', 'inner', 'outer')), may hold values from -11 to 11
- keys: bfloat16 [8192, 512], P(('head', 'inner', 'outer')), may hold values from -11 to 11
- values: bfloat16 [8192, 512], P(('head', 'inner', 'outer')), may hold values from -6 to 6
- outputs: bfloat16 [8192, 4096], P(('head', 'inner', 'outer')), may hold values from -6 to 6
- out_grads: bfloat16 [8192, 4096], P(('head', 'inner', 'outer')), may hold values from -6 to 6
- block_order: int32 [128], replicated, may hold values from 0 to 127, each once
- segment_ids: int32 [8192], replicated, may hold values from 0 to 3, never falling along the last dimension, each value on 1 to 4096 neighbouring positions
Outputs:
- grad_queries: bfloat16 [8192, 4096], P(('head', 'inner', 'outer'))
- grad_keys: bfloat16 [8192, 512], P(('head', 'inner', 'outer'))
- grad_values: bfloat16 [8192, 512], P(('head', 'inner', 'outer'))
Inputs may be any that keep to these rules, and one draw needn't show every extreme that they name: `block_order`: a permutation of the 128 position blocks. `segment_ids`: document numbers never fall along positions; each document has 1 to 4096 positions, one exactly 4096.
All inputs are finite; a program needn't handle non-finite values.
Results may differ from a plain program's by a relative error of at most 0.0049.
Values may be sent and summed in bfloat16 or wider, within the bound.
No kernel may reach another device: no remote copies, remote signals or barrier semaphores. Data moves between devices by JAX's collectives and lax.ppermute only.
A program may use at most 64 MiB of HBM per device.

v0:
```python
import math

import jax
import jax.numpy as jnp
from jax import lax
from jax.experimental import pallas as pl
from jax.experimental.pallas import tpu as pltpu
from jax.sharding import Mesh, PartitionSpec as P

HQ = 32
KVH = 4
DH = 128
ROWS = 64
SEQ = 8192
BLOCKS = 128
DOCS = 4
DOC_MOST = 4096
SLOTS = 8
HEADS = 4
LANES = HEADS * ROWS
TILE = 1024
TILES = (DOC_MOST + ROWS) // TILE + 2
RUN = 8
PIECE = RUN * ROWS

SCALE = 1.0 / math.sqrt(DH)
LOG2E = 1.0 / math.log(2.0)

AXES = ("yl", "c", "yh", "x", "z")
SIZES = (2, 2, 2, 4, 4)
YC = ("yh", "yl", "c")
Y = ("yh", "yl")


def stored_block(yl, c, yh, x, z):
    return (((yl * 2 + c) * 2 + yh) * 4 + x) * 4 + z


def block_rows(index):
    return pl.ds(pl.multiple_of(index * ROWS, ROWS), ROWS)


def attend_kernel(*refs):
    order_ref, seg_ref, qg_ref = refs[:3]
    pieces = refs[3:19]
    dq_ref, mine, other = refs[19], refs[20:28], refs[28:36]
    kv_ref, dk_acc, dv_acc, e_ref, qt_ref, gt_ref, q_ref, g_ref, dqt_ref, sem = refs[36:]
    c, x, z = lax.axis_index("c"), lax.axis_index("x"), lax.axis_index("z")

    def place_of(core, yh, far, i):
        near, yl = i // 2, i % 2
        sx, sz = (far, near) if yh == 0 else (near, far)
        sc = c if core == 0 else 1 - c
        return sc, yl, sx, sz

    def load(i, _):
        for core in range(2):
            for yh in range(2):
                for n in range(4):
                    sc, yl, sx, sz = place_of(core, yh, n, i)
                    place = order_ref[stored_block(yl, sc, yh, (x + 4 - sx) % 4, (z + 4 - sz) % 4)]
                    pltpu.make_async_copy(
                        pieces[(core * 2 + yh) * 4 + n].at[block_rows(i)],
                        kv_ref.at[block_rows(place)],
                        sem,
                    ).start()
        return 0

    lax.fori_loop(0, RUN, load, 0)

    kv_ref[SEQ:, :] = jnp.zeros((TILE, 2 * DH), jnp.bfloat16)
    dk_acc[...] = jnp.zeros_like(dk_acc)
    dv_acc[...] = jnp.zeros_like(dv_acc)
    seg = seg_ref[...]
    starts = [jnp.sum((seg < d).astype(jnp.int32)) for d in range(1, DOCS)]

    lane = lax.broadcasted_iota(jnp.int32, (1, LANES), 1)
    row_in_block = lane % ROWS
    tile_row = lax.broadcasted_iota(jnp.int32, (TILE, LANES), 0)
    whole = kv_ref.at[pl.ds(0, SEQ)]
    pltpu.make_async_copy(whole, whole, sem).wait()

    def one_slot(s, _):
        place = order_ref[stored_block((s // 2) % 2, s % 2, s // 4, x, z)]
        first = place * ROWS
        lo = jnp.int32(0)
        lo_last = jnp.int32(0)
        row_pos = first + row_in_block
        row_lo = jnp.zeros((1, LANES), jnp.int32)
        for start in starts:
            lo = jnp.where(start <= first, start, lo)
            lo_last = jnp.where(start <= first + ROWS - 1, start, lo_last)
            row_lo = jnp.where(start <= row_pos, start, row_lo)
        base = lo // ROWS * ROWS
        count = (first + ROWS - base + TILE - 1) // TILE
        inner_lo = jnp.minimum((lo_last - base + TILE - 1) // TILE, count)
        inner_hi = jnp.maximum((first - base) // TILE, inner_lo)
        for h in range(HEADS):
            q_ref[h * ROWS:(h + 1) * ROWS, :] = qg_ref[s, :, h * DH:(h + 1) * DH]
            g_ref[h * ROWS:(h + 1) * ROWS, :] = qg_ref[s, :, (HEADS + h) * DH:(HEADS + h + 1) * DH]
        qt_ref[...] = q_ref[...].T
        gt_ref[...] = g_ref[...].T
        parts = qg_ref[s, :16, 2 * HEADS * DH:].astype(jnp.float32)
        delta = jnp.concatenate(
            [parts[i:i + 1] + parts[i + 2:i + 3] + parts[i + 4:i + 5] for i in range(2)], axis=1
        )

        def rows_of(t):
            return pl.ds(pl.multiple_of(base + t * TILE, ROWS), TILE)

        def kept(t):
            return pl.ds(pl.multiple_of(t * TILE, TILE), TILE)

        def scores(masked):
            def step(t, top):
                st = jnp.dot(
                    kv_ref[rows_of(t), :DH], qt_ref[...], preferred_element_type=jnp.float32
                ) * (SCALE * LOG2E)
                if masked:
                    pos = tile_row + (base + t * TILE)
                    st = jnp.where((pos <= row_pos) & (pos >= row_lo), st, -2e30)
                e_ref[kept(t), :] = st
                return jnp.maximum(top, jnp.max(st.reshape(TILE // 8, 8, LANES), axis=0))
            return step

        top = jnp.full((8, LANES), -1e30, jnp.float32)
        top = lax.fori_loop(0, inner_lo, scores(True), top)
        top = lax.fori_loop(inner_lo, inner_hi, scores(False), top)
        top = lax.fori_loop(inner_hi, count, scores(True), top)
        top = jnp.max(top, axis=0, keepdims=True)

        def exps(t, total):
            e = jnp.exp2(e_ref[kept(t), :] - top)
            e_ref[kept(t), :] = e
            return total + jnp.sum(e.reshape(TILE // 8, 8, LANES), axis=0)

        total = lax.fori_loop(0, count, exps, jnp.zeros((8, LANES), jnp.float32))
        inverse = 1.0 / jnp.sum(total, axis=0, keepdims=True)
        dqt_ref[...] = jnp.zeros_like(dqt_ref)

        def grads(t, _):
            p = e_ref[kept(t), :] * inverse
            dp = jnp.dot(kv_ref[rows_of(t), DH:], gt_ref[...], preferred_element_type=jnp.float32)
            pb = p.astype(jnp.bfloat16)
            ds = (p * (dp - delta) * SCALE).astype(jnp.bfloat16)
            dv_acc[rows_of(t), :] += jnp.dot(pb, g_ref[...], preferred_element_type=jnp.float32)
            dk_acc[rows_of(t), :] += jnp.dot(ds, q_ref[...], preferred_element_type=jnp.float32)
            dqt_ref[...] += lax.dot_general(
                kv_ref[rows_of(t), :DH], ds, (((0,), (0,)), ((), ())),
                preferred_element_type=jnp.float32,
            )
            return 0

        lax.fori_loop(0, count, grads, 0)
        dq = dqt_ref[...].T.astype(jnp.bfloat16)
        for h in range(HEADS):
            dq_ref[s, :, h * DH:(h + 1) * DH] = dq[h * ROWS:(h + 1) * ROWS, :]
        return 0

    lax.fori_loop(0, SLOTS, one_slot, 0)

    def store(i, _):
        for core in range(2):
            for yh in range(2):
                for n in range(4):
                    sc, yl, sx, sz = place_of(core, yh, n, i)
                    place = order_ref[stored_block(yl, sc, yh, (x + sx) % 4, (z + sz) % 4)]
                    out = (mine if core == 0 else other)[yh * 4 + n]
                    out[block_rows(i), :DH] = dk_acc[block_rows(place), :].astype(out.dtype)
                    out[block_rows(i), DH:] = dv_acc[block_rows(place), :].astype(out.dtype)
        return 0

    lax.fori_loop(0, RUN, store, 0)


def attend(order, seg, qg, pieces):
    vmem = pl.BlockSpec(memory_space=pltpu.VMEM)
    piece = (PIECE, 2 * DH)
    result = pl.pallas_call(
        attend_kernel,
        out_shape=(
            jax.ShapeDtypeStruct((SLOTS, ROWS, HEADS * DH), jnp.bfloat16),
        )
        + (jax.ShapeDtypeStruct(piece, jnp.float32),) * 8
        + (jax.ShapeDtypeStruct(piece, jnp.bfloat16),) * 8,
        in_specs=[pl.BlockSpec(memory_space=pltpu.SMEM), vmem, vmem]
        + [pl.BlockSpec(memory_space=pltpu.HBM)] * 16,
        out_specs=(vmem,) * 17,
        scratch_shapes=[
            pltpu.VMEM((SEQ + TILE, 2 * DH), jnp.bfloat16),
            pltpu.VMEM((SEQ + TILE, DH), jnp.float32),
            pltpu.VMEM((SEQ + TILE, DH), jnp.float32),
            pltpu.VMEM((TILES * TILE, LANES), jnp.float32),
            pltpu.VMEM((DH, LANES), jnp.bfloat16),
            pltpu.VMEM((DH, LANES), jnp.bfloat16),
            pltpu.VMEM((LANES, DH), jnp.bfloat16),
            pltpu.VMEM((LANES, DH), jnp.bfloat16),
            pltpu.VMEM((DH, LANES), jnp.float32),
            pltpu.SemaphoreType.DMA,
        ],
        compiler_params=pltpu.CompilerParams(vmem_limit_bytes=48 * 1024 * 1024),
        cost_estimate=pl.CostEstimate(
            flops=8 * 10**9, bytes_accessed=12 * 10**6, transcendentals=8 * 10**6
        ),
        name="attend",
    )(order, seg, qg, *pieces)
    return result[0], result[1:9], result[9:]


def exchange(value, axes):
    return lax.all_to_all(value, axes, split_axis=0, concat_axis=0, tiled=True)


def ahead(value, axis, n):
    return lax.ppermute(value, axis, [(i, (i + n) % 4) for i in range(4)])


def other_core(value):
    return lax.ppermute(value, "c", [(0, 1), (1, 0)])


def added(terms):
    return sum(term.astype(jnp.float32) for term in terms)


def per_device(queries, keys, values, outputs, out_grads, block_order, segment_ids):
    kv = jnp.concatenate(
        [keys.reshape(ROWS, KVH, DH), values.reshape(ROWS, KVH, DH)], axis=-1
    ).transpose(1, 0, 2).reshape(KVH * ROWS, 2 * DH)
    kv = exchange(kv, Y)
    ways = (("z", "x"), ("x", "z"))
    halves = [kv[yh * 2 * ROWS:(yh + 1) * 2 * ROWS] for yh in range(2)]
    runs = [
        jnp.concatenate([half] + [ahead(half, way[0], n) for n in (1, 2, 3)], axis=0)
        for half, way in zip(halves, ways)
    ]
    runs = lax.optimization_barrier(runs)
    pieces = []
    for run, way in zip(runs, ways):
        pieces += [run] + [ahead(run, way[1], n) for n in (1, 2, 3)]
    pieces += [other_core(piece) for piece in pieces]

    products = outputs.astype(jnp.float32) * out_grads.astype(jnp.float32)
    delta = jnp.sum(products.reshape(ROWS, HQ, DH), axis=-1).T.reshape(SLOTS, 2, DH)
    high = lax.reduce_precision(delta, 8, 7)
    middle = lax.reduce_precision(delta - high, 8, 7)
    low = delta - high - middle
    parts = jnp.concatenate([high, middle, low], axis=1).astype(jnp.bfloat16)
    qg = jnp.concatenate(
        [
            queries.reshape(ROWS, SLOTS, HEADS * DH).transpose(1, 0, 2),
            out_grads.reshape(ROWS, SLOTS, HEADS * DH).transpose(1, 0, 2),
            jnp.pad(parts, ((0, 0), (0, ROWS - 6), (0, 0))),
        ],
        axis=-1,
    )
    qg = exchange(qg, YC)

    dq, mine, other = attend(block_order, segment_ids.reshape(SEQ // 128, 128), qg, pieces)

    back = (("x", "z"), ("z", "x"))
    both = [None] * 8
    for i in (1, 5, 3, 7, 2, 6, 0, 4):
        both[i] = (mine[i] + other_core(other[i]).astype(jnp.float32)).astype(jnp.bfloat16)
    parts = []
    for yh, way in enumerate(back):
        own, *sent = both[yh * 4:yh * 4 + 4]
        terms = [own] + [ahead(term, way[0], n) for n, term in zip((1, 2, 3), sent)]
        parts.append(added(terms).astype(jnp.bfloat16).reshape(4, 2 * ROWS, 2 * DH))
    parts = lax.optimization_barrier(parts)
    sums = []
    for part, way in zip(parts, back):
        terms = [part[0]] + [ahead(part[n], way[1], n) for n in (1, 2, 3)]
        sums.append(added(terms).astype(jnp.bfloat16))
    sums = exchange(jnp.concatenate(sums, axis=0), Y).reshape(KVH, ROWS, 2, DH)
    grad_keys = sums[:, :, 0].transpose(1, 0, 2).reshape(ROWS, KVH * DH)
    grad_values = sums[:, :, 1].transpose(1, 0, 2).reshape(ROWS, KVH * DH)
    grad_queries = exchange(dq, YC).transpose(1, 0, 2).reshape(ROWS, HQ * DH)
    return grad_queries, grad_keys, grad_values


def solution(mesh):
    split = Mesh(mesh.devices.reshape(SIZES), AXES)
    rows = P(AXES, None)
    return jax.shard_map(
        per_device,
        mesh=split,
        in_specs=(rows, rows, rows, rows, rows, P(), P()),
        out_specs=(rows, rows, rows),
        check_vma=False,
    )
```

profile of v0, /device:TPU:0, one launch (start us, length us, event | category | flops | bytes accessed | tf_op | source)
XLA Modules:
  0.0 167.3 jit_solution(8704410474198406361)
XLA Ops:
  0.6 0.8 copy-done
  1.5 0.9 copy_bitcast_fusion.2
  3.0 4.5 %all-to-all-start.1 = ((bf16[4,64,256]{2,1,0:T(8,128)(2,1)}), bf16[4,64,256]{2,1,0:T(8,128)(2,1)S(1)}, u32[]{:S(2)}, u32[]{:S(2)}) async-start(bf16[4,64,256]{2,1,0:T(8,128)(2,1)} %maximum_bitcast_fusion), calls=%async_computation.1 | async-start | bytes 262144 | tf_op jit(solution)/shard_map/all_to_all | solution.py:211
  7.6 1.3 multiply_bitcast_fusion
  10.2 3.3 %all-to-all-done.1 = bf16[4,64,256]{2,1,0:T(8,128)(2,1)S(1)} async-done(((bf16[4,64,256]{2,1,0:T(8,128)(2,1)}), bf16[4,64,256]{2,1,0:T(8,128)(2,1)S(1)}, u32[]{:S(2)}, u32[]{:S(2)}) %all-to-all-start.1) | async-done | bytes 131104 | tf_op jit(solution)/shard_map/all_to_all | solution.py:211
  13.6 4.1 %collective-permute-start.2 = (bf16[128,256]{1,0:T(8,128)(2,1)S(1)}, bf16[128,256]{1,0:T(8,128)(2,1)S(1)}, u32[]{:S(2)}, u32[]{:S(2)}) collective-permute-start(bf16[128,256]{1,0:T(8,128)(2,1)S(1)} %bitcast.83), channel_id=1, source_target_pairs={{0,3},{1,0},{2,1},{3,2},{4,7},{5,4},{6,5},{7,6},{8,11},{9,8},{10,9... | collective-permute-start | bytes 196616 | tf_op jit(solution)/shard_map/ppermute | solution.py:215
  17.7 1.3 collective-permute-start
  18.9 1.2 pad_maximum_fusion
  20.1 4.4 %all-to-all-start = ((bf16[8,64,1152]{2,1,0:T(8,128)(2,1)}), bf16[8,64,1152]{2,1,0:T(8,128)(2,1)}, u32[]{:S(2)}, u32[]{:S(2)}) async-start(bf16[8,64,1152]{2,1,0:T(8,128)(2,1)} %pad_maximum_fusion), calls=%async_computation | async-start | bytes 2359296 | tf_op jit(solution)/shard_map/all_to_all | solution.py:211
  24.5 2.8 %collective-permute-start.5 = (bf16[128,256]{1,0:T(8,128)(2,1)S(1)}, bf16[128,256]{1,0:T(8,128)(2,1)S(1)}, u32[]{:S(2)}, u32[]{:S(2)}) collective-permute-start(bf16[128,256]{1,0:T(8,128)(2,1)S(1)} %bitcast.79), channel_id=1, source_target_pairs={{0,12},{4,0},{8,4},{12,8},{1,13},{5,1},{9,5},{13,9},{2,14},{6,2},{... | collective-permute-start | bytes 196616 | tf_op jit(solution)/shard_map/ppermute | solution.py:215
  27.3 0.8 collective-permute-start.4
  28.1 0.9 collective-permute-start.3
  29.0 1.5 collective-permute-done.5
  30.6 3.0 %collective-permute-done.4 = bf16[128,256]{1,0:T(8,128)(2,1)S(1)} collective-permute-done((bf16[128,256]{1,0:T(8,128)(2,1)S(1)}, bf16[128,256]{1,0:T(8,128)(2,1)S(1)}, u32[]{:S(2)}, u32[]{:S(2)}) %collective-permute-start.4) | collective-permute-done | bytes 65568 | tf_op jit(solution)/shard_map/ppermute | solution.py:215
  35.0 0.8 collective-permute-start.7
  35.8 1.1 collective-permute-start.6
  36.9 2.0 %collective-permute-start.11 = (bf16[512,256]{1,0:T(8,128)(2,1)S(1)}, bf16[512,256]{1,0:T(8,128)(2,1)S(1)}, u32[]{:S(2)}, u32[]{:S(2)}) collective-permute-start(bf16[512,256]{1,0:T(8,128)(2,1)S(1)} %pad_maximum_fusion.2.refs_7_), channel_id=1, source_target_pairs={{0,3},{1,0},{2,1},{3,2},{4,7},{5,4},{6,5},{7,6},{8,11},{9,8},{10,9... | collective-permute-start | bytes 786440 | tf_op jit(solution)/shard_map/ppermute | solution.py:215
  38.9 4.7 %collective-permute-done.8.refs_6_ = bf16[512,256]{1,0:T(8,128)(2,1)S(1)} collective-permute-done((bf16[512,256]{1,0:T(8,128)(2,1)S(1)}, bf16[512,256]{1,0:T(8,128)(2,1)S(1)}, u32[]{:S(2)}, u32[]{:S(2)}) %collective-permute-start.8) | collective-permute-done | bytes 262176 | tf_op jit(solution)/shard_map/ppermute | solution.py:215
  43.6 2.3 %collective-permute-start.10 = (bf16[512,256]{1,0:T(8,128)(2,1)S(1)}, bf16[512,256]{1,0:T(8,128)(2,1)S(1)}, u32[]{:S(2)}, u32[]{:S(2)}) collective-permute-start(bf16[512,256]{1,0:T(8,128)(2,1)S(1)} %pad_maximum_fusion.2.refs_7_), channel_id=1, source_target_pairs={{0,2},{1,3},{2,0},{3,1},{4,6},{5,7},{6,4},{7,5},{8,10},{9,11},{10,... | collective-permute-start | bytes 786440 | tf_op jit(solution)/shard_map/ppermute | solution.py:215
  45.8 2.1 %collective-permute-start.9 = (bf16[512,256]{1,0:T(8,128)(2,1)S(1)}, bf16[512,256]{1,0:T(8,128)(2,1)S(1)}, u32[]{:S(2)}, u32[]{:S(2)}) collective-permute-start(bf16[512,256]{1,0:T(8,128)(2,1)S(1)} %pad_maximum_fusion.2.refs_7_), channel_id=1, source_target_pairs={{0,1},{1,2},{2,3},{3,0},{4,5},{5,6},{6,7},{7,4},{8,9},{9,10},{10,1... | collective-permute-start | bytes 786440 | tf_op jit(solution)/shard_map/ppermute | solution.py:215
  47.9 2.6 %collective-permute-done.6.refs_4_ = bf16[512,256]{1,0:T(8,128)(2,1)S(1)} collective-permute-done((bf16[512,256]{1,0:T(8,128)(2,1)S(1)}, bf16[512,256]{1,0:T(8,128)(2,1)S(1)}, u32[]{:S(2)}, u32[]{:S(2)}) %collective-permute-start.6) | collective-permute-done | bytes 262176 | tf_op jit(solution)/shard_map/ppermute | solution.py:215
  51.1 3.2 %collective-permute-done.10.refs_9_ = bf16[512,256]{1,0:T(8,128)(2,1)S(1)} collective-permute-done((bf16[512,256]{1,0:T(8,128)(2,1)S(1)}, bf16[512,256]{1,0:T(8,128)(2,1)S(1)}, u32[]{:S(2)}, u32[]{:S(2)}) %collective-permute-start.10) | collective-permute-done | bytes 262176 | tf_op jit(solution)/shard_map/ppermute | solution.py:215
  54.4 3.7 %collective-permute-done.9.refs_8_ = bf16[512,256]{1,0:T(8,128)(2,1)S(1)} collective-permute-done((bf16[512,256]{1,0:T(8,128)(2,1)S(1)}, bf16[512,256]{1,0:T(8,128)(2,1)S(1)}, u32[]{:S(2)}, u32[]{:S(2)}) %collective-permute-start.9) | collective-permute-done | bytes 262176 | tf_op jit(solution)/shard_map/ppermute | solution.py:215
  61.4 0.7 copy-done.11
  62.1 0.7 copy-done.13
  62.9 0.9 copy-done.2
  63.8 0.9 copy-done.5
  64.8 0.9 copy-done.7
  65.7 0.9 copy-done.10
  66.7 0.9 copy-done.12
  67.6 0.9 copy-done.14
  68.6 38.0 %attend.1 = (bf16[8,64,512]{2,1,0:T(8,128)(2,1)}, f32[512,256]{1,0:T(8,128)}, f32[512,256]{1,0:T(8,128)}, f32[512,256]{1,0:T(8,128)}, f32[512,256]{1,0:T(8,128)}...) custom-call(s32[128]{0:T(128)S(1)} %copy-done.16, ...), custom_call_target="tpu_custom_call" | custom-call | flops 8000000000 | bytes 12000000 | tf_op jit(solution)/shard_map/attend/pallas_call | solution.py:179
  106.6 0.7 copy-done.3
  107.3 0.7 copy-done.8
  108.6 4.5 %all-to-all-start.2 = ((bf16[8,64,512]{2,1,0:T(8,128)(2,1)}), bf16[8,64,512]{2,1,0:T(8,128)(2,1)S(1)}, u32[]{:S(2)}, u32[]{:S(2)}) async-start(bf16[8,64,512]{2,1,0:T(8,128)(2,1)} %get-tuple-element.26), calls=%async_computation.2 | async-start | bytes 1048576 | tf_op jit(solution)/shard_map/all_to_all | solution.py:211
  114.2 1.0 add_convert_fusion.8
  115.7 1.0 add_convert_fusion.7
  117.1 3.3 %collective-permute-start.26 = (bf16[512,256]{1,0:T(8,128)(2,1)S(1)}, bf16[512,256]{1,0:T(8,128)(2,1)S(1)}, u32[]{:S(2)}, u32[]{:S(2)}) collective-permute-start(bf16[512,256]{1,0:T(8,128)(2,1)S(1)} %add_convert_fusion.6), channel_id=1, source_target_pairs={{0,12},{4,0},{8,4},{12,8},{1,13},{5,1},{9,5},{13,9},{2,14},{6,2},{... | collective-permute-start | bytes 786440 | tf_op jit(solution)/shard_map/ppermute | solution.py:215
  120.7 11.2 %collective-permute-done.22 = bf16[512,256]{1,0:T(8,128)(2,1)S(1)} collective-permute-done((bf16[512,256]{1,0:T(8,128)(2,1)S(1)}, bf16[512,256]{1,0:T(8,128)(2,1)S(1)}, u32[]{:S(2)}, u32[]{:S(2)}) %collective-permute-start.22) | collective-permute-done | bytes 262176 | tf_op jit(solution)/shard_map/ppermute | solution.py:215
  131.9 0.8 collective-permute-done.26
  132.9 8.3 %collective-permute-done.31 = bf16[512,256]{1,0:T(8,128)(2,1)S(1)} collective-permute-done((bf16[512,256]{1,0:T(8,128)(2,1)S(1)}, bf16[512,256]{1,0:T(8,128)(2,1)S(1)}, u32[]{:S(2)}, u32[]{:S(2)}) %collective-permute-start.31) | collective-permute-done | bytes 262176 | tf_op jit(solution)/shard_map/ppermute | solution.py:215
  141.4 3.2 %collective-permute-start.36 = (bf16[128,256]{1,0:T(8,128)(2,1)S(1)}, bf16[128,256]{1,0:T(8,128)(2,1)S(1)}, u32[]{:S(2)}, u32[]{:S(2)}) collective-permute-start(bf16[128,256]{1,0:T(8,128)(2,1)S(1)} %get-tuple-element.46), channel_id=1, source_target_pairs={{0,3},{1,0},{2,1},{3,2},{4,7},{5,4},{6,5},{7,6},{8,11},{9,8},{10,9... | collective-permute-start | bytes 196616 | tf_op jit(solution)/shard_map/ppermute | solution.py:215
  145.3 3.2 %collective-permute-start.39 = (bf16[128,256]{1,0:T(8,128)(2,1)S(1)}, bf16[128,256]{1,0:T(8,128)(2,1)S(1)}, u32[]{:S(2)}, u32[]{:S(2)}) collective-permute-start(bf16[128,256]{1,0:T(8,128)(2,1)S(1)} %get-tuple-element.49), channel_id=1, source_target_pairs={{0,12},{4,0},{8,4},{12,8},{1,13},{5,1},{9,5},{13,9},{2,14},{6,2},{... | collective-permute-start | bytes 196616 | tf_op jit(solution)/shard_map/ppermute | solution.py:215
  148.5 1.9 %collective-permute-done.35 = bf16[128,256]{1,0:T(8,128)(2,1)S(1)} collective-permute-done((bf16[128,256]{1,0:T(8,128)(2,1)S(1)}, bf16[128,256]{1,0:T(8,128)(2,1)S(1)}, u32[]{:S(2)}, u32[]{:S(2)}) %collective-permute-start.35) | collective-permute-done | bytes 65568 | tf_op jit(solution)/shard_map/ppermute | solution.py:215
  151.1 3.3 %collective-permute-done.38 = bf16[128,256]{1,0:T(8,128)(2,1)S(1)} collective-permute-done((bf16[128,256]{1,0:T(8,128)(2,1)S(1)}, bf16[128,256]{1,0:T(8,128)(2,1)S(1)}, u32[]{:S(2)}, u32[]{:S(2)}) %collective-permute-start.38) | collective-permute-done | bytes 65568 | tf_op jit(solution)/shard_map/ppermute | solution.py:215
  155.0 4.8 %all-to-all-start.3 = ((bf16[4,64,256]{2,1,0:T(8,128)(2,1)}), bf16[4,64,256]{2,1,0:T(8,128)(2,1)S(1)}, u32[]{:S(2)}, u32[]{:S(2)}) async-start(bf16[4,64,256]{2,1,0:T(8,128)(2,1)} %bitcast.18), calls=%async_computation.3 | async-start | bytes 262144 | tf_op jit(solution)/shard_map/all_to_all | solution.py:211
  159.8 0.8 copy.46
  160.6 5.1 %all-to-all-done.3 = bf16[4,64,256]{2,1,0:T(8,128)(2,1)S(1)} async-done(((bf16[4,64,256]{2,1,0:T(8,128)(2,1)}), bf16[4,64,256]{2,1,0:T(8,128)(2,1)S(1)}, u32[]{:S(2)}, u32[]{:S(2)}) %all-to-all-start.3) | async-done | bytes 131104 | tf_op jit(solution)/shard_map/all_to_all | solution.py:211
  (129 shorter events, 13.9 us)
Async XLA Ops:
  3.0 10.5 %all-to-all-start.1 = ((bf16[4,64,256]{2,1,0:T(8,128)(2,1)}), bf16[4,64,256]{2,1,0:T(8,128)(2,1)S(1)}, u32[]{:S(2)}, u32[]{:S(2)}) async-start(bf16[4,64,256]{2,1,0:T(8,128)(2,1)} %maximum_bitcast_fusion), calls=%async_computation.1 | async-start | bytes 262144 | tf_op jit(solution)/shard_map/all_to_all | solution.py:211
  13.6 14.6 %collective-permute-start.2 = (bf16[128,256]{1,0:T(8,128)(2,1)S(1)}, bf16[128,256]{1,0:T(8,128)(2,1)S(1)}, u32[]{:S(2)}, u32[]{:S(2)}) collective-permute-start(bf16[128,256]{1,0:T(8,128)(2,1)S(1)} %bitcast.83), channel_id=1, source_target_pairs={{0,3},{1,0},{2,1},{3,2},{4,7},{5,4},{6,5},{7,6},{8,11},{9,8},{10,9... | collective-permute-start | bytes 196616 | tf_op jit(solution)/shard_map/ppermute | solution.py:215
  17.7 11.4 %collective-permute-start.1 = (bf16[128,256]{1,0:T(8,128)(2,1)S(1)}, bf16[128,256]{1,0:T(8,128)(2,1)S(1)}, u32[]{:S(2)}, u32[]{:S(2)}) collective-permute-start(bf16[128,256]{1,0:T(8,128)(2,1)S(1)} %bitcast.84), channel_id=1, source_target_pairs={{0,2},{1,3},{2,0},{3,1},{4,6},{5,7},{6,4},{7,5},{8,10},{9,11},{10,... | collective-permute-start | bytes 196616 | tf_op jit(solution)/shard_map/ppermute | solution.py:215
  17.7 11.4 %collective-permute-start = (bf16[128,256]{1,0:T(8,128)(2,1)S(1)}, bf16[128,256]{1,0:T(8,128)(2,1)S(1)}, u32[]{:S(2)}, u32[]{:S(2)}) collective-permute-start(bf16[128,256]{1,0:T(8,128)(2,1)S(1)} %bitcast.85), channel_id=1, source_target_pairs={{0,1},{1,2},{2,3},{3,0},{4,5},{5,6},{6,7},{7,4},{8,9},{9,10},{10,1... | collective-permute-start | bytes 196616 | tf_op jit(solution)/shard_map/ppermute | solution.py:215
  20.1 42.8 %copy-start.15 = (s32[8192]{0:T(1024)S(1)}, s32[8192]{0:T(1024)}, u32[]{:S(2)}) copy-start(s32[8192]{0:T(1024)} %param.13) | copy-start | bytes 98308
  20.1 42.8 %copy-start.16 = (s32[128]{0:T(128)S(1)}, s32[128]{0:T(128)}, u32[]{:S(2)}) copy-start(s32[128]{0:T(128)} %refs_0_.1) | copy-start | bytes 1540
  20.1 42.8 %all-to-all-start = ((bf16[8,64,1152]{2,1,0:T(8,128)(2,1)}), bf16[8,64,1152]{2,1,0:T(8,128)(2,1)}, u32[]{:S(2)}, u32[]{:S(2)}) async-start(bf16[8,64,1152]{2,1,0:T(8,128)(2,1)} %pad_maximum_fusion), calls=%async_computation | async-start | bytes 2359296 | tf_op jit(solution)/shard_map/all_to_all | solution.py:211
  24.5 6.1 %collective-permute-start.5 = (bf16[128,256]{1,0:T(8,128)(2,1)S(1)}, bf16[128,256]{1,0:T(8,128)(2,1)S(1)}, u32[]{:S(2)}, u32[]{:S(2)}) collective-permute-start(bf16[128,256]{1,0:T(8,128)(2,1)S(1)} %bitcast.79), channel_id=1, source_target_pairs={{0,12},{4,0},{8,4},{12,8},{1,13},{5,1},{9,5},{13,9},{2,14},{6,2},{... | collective-permute-start | bytes 196616 | tf_op jit(solution)/shard_map/ppermute | solution.py:215
  27.3 6.3 %collective-permute-start.4 = (bf16[128,256]{1,0:T(8,128)(2,1)S(1)}, bf16[128,256]{1,0:T(8,128)(2,1)S(1)}, u32[]{:S(2)}, u32[]{:S(2)}) collective-permute-start(bf16[128,256]{1,0:T(8,128)(2,1)S(1)} %bitcast.80), channel_id=1, source_target_pairs={{0,8},{4,12},{8,0},{12,4},{1,9},{5,13},{9,1},{13,5},{2,10},{6,14},... | collective-permute-start | bytes 196616 | tf_op jit(solution)/shard_map/ppermute | solution.py:215
  28.1 6.1 %collective-permute-start.3 = (bf16[128,256]{1,0:T(8,128)(2,1)S(1)}, bf16[128,256]{1,0:T(8,128)(2,1)S(1)}, u32[]{:S(2)}, u32[]{:S(2)}) collective-permute-start(bf16[128,256]{1,0:T(8,128)(2,1)S(1)} %bitcast.81), channel_id=1, source_target_pairs={{0,4},{4,8},{8,12},{12,0},{1,5},{5,9},{9,13},{13,1},{2,6},{6,10},{... | collective-permute-start | bytes 196616 | tf_op jit(solution)/shard_map/ppermute | solution.py:215
  34.3 2.6 %collective-permute-start.12 = (bf16[512,256]{1,0:T(8,128)(2,1)S(1)}, bf16[512,256]{1,0:T(8,128)(2,1)S(1)}, u32[]{:S(2)}, u32[]{:S(2)}) collective-permute-start(bf16[512,256]{1,0:T(8,128)(2,1)S(1)} %pad_maximum_fusion.1.refs_3_), channel_id=1, source_target_pairs={{0,32},{32,0},{1,33},{33,1},{2,34},{34,2},{3,35},{35,3},{4,36},{36... | collective-permute-start | bytes 786440 | tf_op jit(solution)/shard_map/ppermute | solution.py:219
  34.4 9.2 %collective-permute-start.8 = (bf16[512,256]{1,0:T(8,128)(2,1)S(1)}, bf16[512,256]{1,0:T(8,128)(2,1)S(1)}, u32[]{:S(2)}, u32[]{:S(2)}) collective-permute-start(bf16[512,256]{1,0:T(8,128)(2,1)S(1)} %pad_maximum_fusion.1.refs_3_), channel_id=1, source_target_pairs={{0,12},{4,0},{8,4},{12,8},{1,13},{5,1},{9,5},{13,9},{2,14},{6,2},{... | collective-permute-start | bytes 786440 | tf_op jit(solution)/shard_map/ppermute | solution.py:215
  35.0 10.8 %collective-permute-start.7 = (bf16[512,256]{1,0:T(8,128)(2,1)S(1)}, bf16[512,256]{1,0:T(8,128)(2,1)S(1)}, u32[]{:S(2)}, u32[]{:S(2)}) collective-permute-start(bf16[512,256]{1,0:T(8,128)(2,1)S(1)} %pad_maximum_fusion.1.refs_3_), channel_id=1, source_target_pairs={{0,8},{4,12},{8,0},{12,4},{1,9},{5,13},{9,1},{13,5},{2,10},{6,14},... | collective-permute-start | bytes 786440 | tf_op jit(solution)/shard_map/ppermute | solution.py:215
  35.8 14.7 %collective-permute-start.6 = (bf16[512,256]{1,0:T(8,128)(2,1)S(1)}, bf16[512,256]{1,0:T(8,128)(2,1)S(1)}, u32[]{:S(2)}, u32[]{:S(2)}) collective-permute-start(bf16[512,256]{1,0:T(8,128)(2,1)S(1)} %pad_maximum_fusion.1.refs_3_), channel_id=1, source_target_pairs={{0,4},{4,8},{8,12},{12,0},{1,5},{5,9},{9,13},{13,1},{2,6},{6,10},{... | collective-permute-start | bytes 786440 | tf_op jit(solution)/shard_map/ppermute | solution.py:215
  36.9 13.6 %collective-permute-start.16 = (bf16[512,256]{1,0:T(8,128)(2,1)S(1)}, bf16[512,256]{1,0:T(8,128)(2,1)S(1)}, u32[]{:S(2)}, u32[]{:S(2)}) collective-permute-start(bf16[512,256]{1,0:T(8,128)(2,1)S(1)} %pad_maximum_fusion.2.refs_7_), channel_id=1, source_target_pairs={{0,32},{32,0},{1,33},{33,1},{2,34},{34,2},{3,35},{35,3},{4,36},{36... | collective-permute-start | bytes 786440 | tf_op jit(solution)/shard_map/ppermute | solution.py:219
  36.9 14.1 %collective-permute-start.11 = (bf16[512,256]{1,0:T(8,128)(2,1)S(1)}, bf16[512,256]{1,0:T(8,128)(2,1)S(1)}, u32[]{:S(2)}, u32[]{:S(2)}) collective-permute-start(bf16[512,256]{1,0:T(8,128)(2,1)S(1)} %pad_maximum_fusion.2.refs_7_), channel_id=1, source_target_pairs={{0,3},{1,0},{2,1},{3,2},{4,7},{5,4},{6,5},{7,6},{8,11},{9,8},{10,9... | collective-permute-start | bytes 786440 | tf_op jit(solution)/shard_map/ppermute | solution.py:215
  43.6 10.8 %collective-permute-start.10 = (bf16[512,256]{1,0:T(8,128)(2,1)S(1)}, bf16[512,256]{1,0:T(8,128)(2,1)S(1)}, u32[]{:S(2)}, u32[]{:S(2)}) collective-permute-start(bf16[512,256]{1,0:T(8,128)(2,1)S(1)} %pad_maximum_fusion.2.refs_7_), channel_id=1, source_target_pairs={{0,2},{1,3},{2,0},{3,1},{4,6},{5,7},{6,4},{7,5},{8,10},{9,11},{10,... | collective-permute-start | bytes 786440 | tf_op jit(solution)/shard_map/ppermute | solution.py:215
  45.8 12.2 %collective-permute-start.9 = (bf16[512,256]{1,0:T(8,128)(2,1)S(1)}, bf16[512,256]{1,0:T(8,128)(2,1)S(1)}, u32[]{:S(2)}, u32[]{:S(2)}) collective-permute-start(bf16[512,256]{1,0:T(8,128)(2,1)S(1)} %pad_maximum_fusion.2.refs_7_), channel_id=1, source_target_pairs={{0,1},{1,2},{2,3},{3,0},{4,5},{5,6},{6,7},{7,4},{8,9},{9,10},{10,1... | collective-permute-start | bytes 786440 | tf_op jit(solution)/shard_map/ppermute | solution.py:215
  50.5 7.6 %collective-permute-start.15 = (bf16[512,256]{1,0:T(8,128)(2,1)S(1)}, bf16[512,256]{1,0:T(8,128)(2,1)S(1)}, u32[]{:S(2)}, u32[]{:S(2)}) collective-permute-start(bf16[512,256]{1,0:T(8,128)(2,1)S(1)} %collective-permute-done.8.refs_6_), channel_id=1, source_target_pairs={{0,32},{32,0},{1,33},{33,1},{2,34},{34,2},{3,35},{35,3},{4,36},{36... | collective-permute-start | bytes 786440 | tf_op jit(solution)/shard_map/ppermute | solution.py:219
  50.5 9.5 %collective-permute-start.14 = (bf16[512,256]{1,0:T(8,128)(2,1)S(1)}, bf16[512,256]{1,0:T(8,128)(2,1)S(1)}, u32[]{:S(2)}, u32[]{:S(2)}) collective-permute-start(bf16[512,256]{1,0:T(8,128)(2,1)S(1)} %collective-permute-done.7.refs_5_), channel_id=1, source_target_pairs={{0,32},{32,0},{1,33},{33,1},{2,34},{34,2},{3,35},{35,3},{4,36},{36... | collective-permute-start | bytes 786440 | tf_op jit(solution)/shard_map/ppermute | solution.py:219
  51.0 9.7 %collective-permute-start.13 = (bf16[512,256]{1,0:T(8,128)(2,1)S(1)}, bf16[512,256]{1,0:T(8,128)(2,1)S(1)}, u32[]{:S(2)}, u32[]{:S(2)}) collective-permute-start(bf16[512,256]{1,0:T(8,128)(2,1)S(1)} %collective-permute-done.6.refs_4_), channel_id=1, source_target_pairs={{0,32},{32,0},{1,33},{33,1},{2,34},{34,2},{3,35},{35,3},{4,36},{36... | collective-permute-start | bytes 786440 | tf_op jit(solution)/shard_map/ppermute | solution.py:219
  54.3 7.0 %collective-permute-start.19 = (bf16[512,256]{1,0:T(8,128)(2,1)S(1)}, bf16[512,256]{1,0:T(8,128)(2,1)S(1)}, u32[]{:S(2)}, u32[]{:S(2)}) collective-permute-start(bf16[512,256]{1,0:T(8,128)(2,1)S(1)} %collective-permute-done.11.refs_10_), channel_id=1, source_target_pairs={{0,32},{32,0},{1,33},{33,1},{2,34},{34,2},{3,35},{35,3},{4,36},{36... | collective-permute-start | bytes 786440 | tf_op jit(solution)/shard_map/ppermute | solution.py:219
  58.1 3.3 %collective-permute-start.18 = (bf16[512,256]{1,0:T(8,128)(2,1)S(1)}, bf16[512,256]{1,0:T(8,128)(2,1)S(1)}, u32[]{:S(2)}, u32[]{:S(2)}) collective-permute-start(bf16[512,256]{1,0:T(8,128)(2,1)S(1)} %collective-permute-done.10.refs_9_), channel_id=1, source_target_pairs={{0,32},{32,0},{1,33},{33,1},{2,34},{34,2},{3,35},{35,3},{4,36},{36... | collective-permute-start | bytes 786440 | tf_op jit(solution)/shard_map/ppermute | solution.py:219
  58.8 3.3 %collective-permute-start.17 = (bf16[512,256]{1,0:T(8,128)(2,1)S(1)}, bf16[512,256]{1,0:T(8,128)(2,1)S(1)}, u32[]{:S(2)}, u32[]{:S(2)}) collective-permute-start(bf16[512,256]{1,0:T(8,128)(2,1)S(1)} %collective-permute-done.9.refs_8_), channel_id=1, source_target_pairs={{0,32},{32,0},{1,33},{33,1},{2,34},{34,2},{3,35},{35,3},{4,36},{36... | collective-permute-start | bytes 786440 | tf_op jit(solution)/shard_map/ppermute | solution.py:219
  108.1 6.0 %collective-permute-start.21 = (bf16[512,256]{1,0:T(8,128)(2,1)}, bf16[512,256]{1,0:T(8,128)(2,1)}, u32[]{:S(2)}, u32[]{:S(2)}) collective-permute-start(bf16[512,256]{1,0:T(8,128)(2,1)} %get-tuple-element.30), channel_id=1, source_target_pairs={{0,32},{32,0},{1,33},{33,1},{2,34},{34,2},{3,35},{35,3},{4,36},{36... | collective-permute-start | bytes 786440 | tf_op jit(solution)/shard_map/ppermute | solution.py:219
  108.1 7.1 %collective-permute-start.23 = (bf16[512,256]{1,0:T(8,128)(2,1)}, bf16[512,256]{1,0:T(8,128)(2,1)}, u32[]{:S(2)}, u32[]{:S(2)}) collective-permute-start(bf16[512,256]{1,0:T(8,128)(2,1)} %get-tuple-element.32), channel_id=1, source_target_pairs={{0,32},{32,0},{1,33},{33,1},{2,34},{34,2},{3,35},{35,3},{4,36},{36... | collective-permute-start | bytes 786440 | tf_op jit(solution)/shard_map/ppermute | solution.py:219
  108.6 46.4 %all-to-all-start.2 = ((bf16[8,64,512]{2,1,0:T(8,128)(2,1)}), bf16[8,64,512]{2,1,0:T(8,128)(2,1)S(1)}, u32[]{:S(2)}, u32[]{:S(2)}) async-start(bf16[8,64,512]{2,1,0:T(8,128)(2,1)} %get-tuple-element.26), calls=%async_computation.2 | async-start | bytes 1048576 | tf_op jit(solution)/shard_map/all_to_all | solution.py:211
  113.1 7.6 %collective-permute-start.20 = (bf16[512,256]{1,0:T(8,128)(2,1)S(1)}, bf16[512,256]{1,0:T(8,128)(2,1)S(1)}, u32[]{:S(2)}, u32[]{:S(2)}) collective-permute-start(bf16[512,256]{1,0:T(8,128)(2,1)S(1)} %get-tuple-element.28), channel_id=1, source_target_pairs={{0,32},{32,0},{1,33},{33,1},{2,34},{34,2},{3,35},{35,3},{4,36},{36... | collective-permute-start | bytes 786440 | tf_op jit(solution)/shard_map/ppermute | solution.py:219
  113.6 3.2 %collective-permute-start.25 = (bf16[512,256]{1,0:T(8,128)(2,1)}, bf16[512,256]{1,0:T(8,128)(2,1)S(1)}, u32[]{:S(2)}, u32[]{:S(2)}) collective-permute-start(bf16[512,256]{1,0:T(8,128)(2,1)} %copy-done.8), channel_id=1, source_target_pairs={{0,32},{32,0},{1,33},{33,1},{2,34},{34,2},{3,35},{35,3},{4,36},{36... | collective-permute-start | bytes 786440 | tf_op jit(solution)/shard_map/ppermute | solution.py:219
  113.6 3.2 %collective-permute-start.28 = (bf16[512,256]{1,0:T(8,128)(2,1)}, bf16[512,256]{1,0:T(8,128)(2,1)S(1)}, u32[]{:S(2)}, u32[]{:S(2)}) collective-permute-start(bf16[512,256]{1,0:T(8,128)(2,1)} %copy-done.3), channel_id=1, source_target_pairs={{0,32},{32,0},{1,33},{33,1},{2,34},{34,2},{3,35},{35,3},{4,36},{36... | collective-permute-start | bytes 786440 | tf_op jit(solution)/shard_map/ppermute | solution.py:219
  114.1 3.0 %collective-permute-start.30 = (bf16[512,256]{1,0:T(8,128)(2,1)S(1)}, bf16[512,256]{1,0:T(8,128)(2,1)S(1)}, u32[]{:S(2)}, u32[]{:S(2)}) collective-permute-start(bf16[512,256]{1,0:T(8,128)(2,1)S(1)} %get-tuple-element.40), channel_id=1, source_target_pairs={{0,32},{32,0},{1,33},{33,1},{2,34},{34,2},{3,35},{35,3},{4,36},{36... | collective-permute-start | bytes 786440 | tf_op jit(solution)/shard_map/ppermute | solution.py:219
  115.2 5.2 %collective-permute-start.32 = (bf16[512,256]{1,0:T(8,128)(2,1)S(1)}, bf16[512,256]{1,0:T(8,128)(2,1)S(1)}, u32[]{:S(2)}, u32[]{:S(2)}) collective-permute-start(bf16[512,256]{1,0:T(8,128)(2,1)S(1)} %get-tuple-element.42), channel_id=1, source_target_pairs={{0,32},{32,0},{1,33},{33,1},{2,34},{34,2},{3,35},{35,3},{4,36},{36... | collective-permute-start | bytes 786440 | tf_op jit(solution)/shard_map/ppermute | solution.py:219
  116.7 15.2 %collective-permute-start.22 = (bf16[512,256]{1,0:T(8,128)(2,1)S(1)}, bf16[512,256]{1,0:T(8,128)(2,1)S(1)}, u32[]{:S(2)}, u32[]{:S(2)}) collective-permute-start(bf16[512,256]{1,0:T(8,128)(2,1)S(1)} %add_convert_fusion.8), channel_id=1, source_target_pairs={{0,4},{4,8},{8,12},{12,0},{1,5},{5,9},{9,13},{13,1},{2,6},{6,10},{... | collective-permute-start | bytes 786440 | tf_op jit(solution)/shard_map/ppermute | solution.py:215
  116.9 15.0 %collective-permute-start.24 = (bf16[512,256]{1,0:T(8,128)(2,1)S(1)}, bf16[512,256]{1,0:T(8,128)(2,1)S(1)}, u32[]{:S(2)}, u32[]{:S(2)}) collective-permute-start(bf16[512,256]{1,0:T(8,128)(2,1)S(1)} %add_convert_fusion.7), channel_id=1, source_target_pairs={{0,8},{4,12},{8,0},{12,4},{1,9},{5,13},{9,1},{13,5},{2,10},{6,14},... | collective-permute-start | bytes 786440 | tf_op jit(solution)/shard_map/ppermute | solution.py:215
  117.1 15.6 %copy-start.19 = (f32[512,256]{1,0:T(8,128)S(1)}, f32[512,256]{1,0:T(8,128)}, u32[]{:S(2)}) copy-start(f32[512,256]{1,0:T(8,128)} %get-tuple-element.27) | copy-start | bytes 1572868
  117.1 15.6 %collective-permute-start.26 = (bf16[512,256]{1,0:T(8,128)(2,1)S(1)}, bf16[512,256]{1,0:T(8,128)(2,1)S(1)}, u32[]{:S(2)}, u32[]{:S(2)}) collective-permute-start(bf16[512,256]{1,0:T(8,128)(2,1)S(1)} %add_convert_fusion.6), channel_id=1, source_target_pairs={{0,12},{4,0},{8,4},{12,8},{1,13},{5,1},{9,5},{13,9},{2,14},{6,2},{... | collective-permute-start | bytes 786440 | tf_op jit(solution)/shard_map/ppermute | solution.py:215
  120.4 12.4 %collective-permute-start.27 = (bf16[512,256]{1,0:T(8,128)(2,1)S(1)}, bf16[512,256]{1,0:T(8,128)(2,1)S(1)}, u32[]{:S(2)}, u32[]{:S(2)}) collective-permute-start(bf16[512,256]{1,0:T(8,128)(2,1)S(1)} %get-tuple-element.36), channel_id=1, source_target_pairs={{0,32},{32,0},{1,33},{33,1},{2,34},{34,2},{3,35},{35,3},{4,36},{36... | collective-permute-start | bytes 786440 | tf_op jit(solution)/shard_map/ppermute | solution.py:219
  120.6 20.6 %copy-start.18 = (f32[512,256]{1,0:T(8,128)S(1)}, f32[512,256]{1,0:T(8,128)}, u32[]{:S(2)}) copy-start(f32[512,256]{1,0:T(8,128)} %get-tuple-element.35) | copy-start | bytes 1572868
  120.6 12.2 %collective-permute-start.29 = (bf16[512,256]{1,0:T(8,128)(2,1)S(1)}, bf16[512,256]{1,0:T(8,128)(2,1)S(1)}, u32[]{:S(2)}, u32[]{:S(2)}) collective-permute-start(bf16[512,256]{1,0:T(8,128)(2,1)S(1)} %add_convert_fusion.3), channel_id=1, source_target_pairs={{0,1},{1,2},{2,3},{3,0},{4,5},{5,6},{6,7},{7,4},{8,9},{9,10},{10,1... | collective-permute-start | bytes 786440 | tf_op jit(solution)/shard_map/ppermute | solution.py:215
  131.9 9.3 %collective-permute-start.31 = (bf16[512,256]{1,0:T(8,128)(2,1)S(1)}, bf16[512,256]{1,0:T(8,128)(2,1)S(1)}, u32[]{:S(2)}, u32[]{:S(2)}) collective-permute-start(bf16[512,256]{1,0:T(8,128)(2,1)S(1)} %add_convert_fusion.2), channel_id=1, source_target_pairs={{0,2},{1,3},{2,0},{3,1},{4,6},{5,7},{6,4},{7,5},{8,10},{9,11},{10,... | collective-permute-start | bytes 786440 | tf_op jit(solution)/shard_map/ppermute | solution.py:215
  131.9 9.3 %collective-permute-start.33 = (bf16[512,256]{1,0:T(8,128)(2,1)S(1)}, bf16[512,256]{1,0:T(8,128)(2,1)S(1)}, u32[]{:S(2)}, u32[]{:S(2)}) collective-permute-start(bf16[512,256]{1,0:T(8,128)(2,1)S(1)} %add_convert_fusion.1), channel_id=1, source_target_pairs={{0,3},{1,0},{2,1},{3,2},{4,7},{5,4},{6,5},{7,6},{8,11},{9,8},{10,9... | collective-permute-start | bytes 786440 | tf_op jit(solution)/shard_map/ppermute | solution.py:215
  141.4 7.2 %collective-permute-start.34 = (bf16[128,256]{1,0:T(8,128)(2,1)S(1)}, bf16[128,256]{1,0:T(8,128)(2,1)S(1)}, u32[]{:S(2)}, u32[]{:S(2)}) collective-permute-start(bf16[128,256]{1,0:T(8,128)(2,1)S(1)} %get-tuple-element.45), channel_id=1, source_target_pairs={{0,1},{1,2},{2,3},{3,0},{4,5},{5,6},{6,7},{7,4},{8,9},{9,10},{10,1... | collective-permute-start | bytes 196616 | tf_op jit(solution)/shard_map/ppermute | solution.py:215
  141.4 7.1 %collective-permute-start.36 = (bf16[128,256]{1,0:T(8,128)(2,1)S(1)}, bf16[128,256]{1,0:T(8,128)(2,1)S(1)}, u32[]{:S(2)}, u32[]{:S(2)}) collective-permute-start(bf16[128,256]{1,0:T(8,128)(2,1)S(1)} %get-tuple-element.46), channel_id=1, source_target_pairs={{0,3},{1,0},{2,1},{3,2},{4,7},{5,4},{6,5},{7,6},{8,11},{9,8},{10,9... | collective-permute-start | bytes 196616 | tf_op jit(solution)/shard_map/ppermute | solution.py:215
  144.7 5.8 %collective-permute-start.35 = (bf16[128,256]{1,0:T(8,128)(2,1)S(1)}, bf16[128,256]{1,0:T(8,128)(2,1)S(1)}, u32[]{:S(2)}, u32[]{:S(2)}) collective-permute-start(bf16[128,256]{1,0:T(8,128)(2,1)S(1)} %get-tuple-element.47), channel_id=1, source_target_pairs={{0,2},{1,3},{2,0},{3,1},{4,6},{5,7},{6,4},{7,5},{8,10},{9,11},{10,... | collective-permute-start | bytes 196616 | tf_op jit(solution)/shard_map/ppermute | solution.py:215
  145.2 5.8 %collective-permute-start.37 = (bf16[128,256]{1,0:T(8,128)(2,1)S(1)}, bf16[128,256]{1,0:T(8,128)(2,1)S(1)}, u32[]{:S(2)}, u32[]{:S(2)}) collective-permute-start(bf16[128,256]{1,0:T(8,128)(2,1)S(1)} %get-tuple-element.48), channel_id=1, source_target_pairs={{0,4},{4,8},{8,12},{12,0},{1,5},{5,9},{9,13},{13,1},{2,6},{6,10},{... | collective-permute-start | bytes 196616 | tf_op jit(solution)/shard_map/ppermute | solution.py:215
  145.3 5.7 %collective-permute-start.39 = (bf16[128,256]{1,0:T(8,128)(2,1)S(1)}, bf16[128,256]{1,0:T(8,128)(2,1)S(1)}, u32[]{:S(2)}, u32[]{:S(2)}) collective-permute-start(bf16[128,256]{1,0:T(8,128)(2,1)S(1)} %get-tuple-element.49), channel_id=1, source_target_pairs={{0,12},{4,0},{8,4},{12,8},{1,13},{5,1},{9,5},{13,9},{2,14},{6,2},{... | collective-permute-start | bytes 196616 | tf_op jit(solution)/shard_map/ppermute | solution.py:215
  148.5 5.8 %collective-permute-start.38 = (bf16[128,256]{1,0:T(8,128)(2,1)S(1)}, bf16[128,256]{1,0:T(8,128)(2,1)S(1)}, u32[]{:S(2)}, u32[]{:S(2)}) collective-permute-start(bf16[128,256]{1,0:T(8,128)(2,1)S(1)} %get-tuple-element.50), channel_id=1, source_target_pairs={{0,8},{4,12},{8,0},{12,4},{1,9},{5,13},{9,1},{13,5},{2,10},{6,14},... | collective-permute-start | bytes 196616 | tf_op jit(solution)/shard_map/ppermute | solution.py:215
  155.0 10.7 %all-to-all-start.3 = ((bf16[4,64,256]{2,1,0:T(8,128)(2,1)}), bf16[4,64,256]{2,1,0:T(8,128)(2,1)S(1)}, u32[]{:S(2)}, u32[]{:S(2)}) async-start(bf16[4,64,256]{2,1,0:T(8,128)(2,1)} %bitcast.18), calls=%async_computation.3 | async-start | bytes 262144 | tf_op jit(solution)/shard_map/all_to_all | solution.py:211
  (24 other events, 42.6 us)
where the time goes:
time: 166 us; the launch traced here: 167 us
  waiting for transfers between devices  53.9 us (32%)
  starting transfers between devices  51 us (31%)
  Pallas kernels  38 us (23%)
  local copies, waits for them, and re-layouts  16.4 us (10%)
  other arithmetic  6.85 us (4%)
    ppermute x24, waiting for transfers between devices, ahead(): return lax.ppermute(value, axis, [(i, (i + n) % 4) for i in range(4)])  45.4 us
    pallas_call x1, Pallas kernels, attend(): pl.pallas_call(attend_kernel, out_shape=(jax.ShapeDtypeStruct((SLOTS, ROW...  38 us
    ppermute x24, starting transfers between devices, ahead(): return lax.ppermute(value, axis, [(i, (i + n) % 4) for i in range(4)])  29.4 us
    all_to_all x4, starting transfers between devices, exchange(): return lax.all_to_all(value, axes, split_axis=0, concat_axis=0, tiled=True)  18.2 us
    unnamed x57, local copies, waits for them, and re-layouts  12.9 us
    all_to_all x4, waiting for transfers between devices, exchange(): return lax.all_to_all(value, axes, split_axis=0, concat_axis=0, tiled=True)  8.45 us
    ppermute x16, starting transfers between devices, other_core(): return lax.ppermute(value, 'c', [(0, 1), (1, 0)])  3.39 us
  transfers between devices with their start and end apart: 44, of which 15 were waited for; matrix products, arithmetic and copies ran while one was open for 4% of the time, Pallas kernels for 0%

commit v1 on v0

v1 whole, which is shorter than its diff:
```python
import math

import jax
import jax.numpy as jnp
from jax import lax
from jax.experimental import pallas as pl
from jax.experimental.pallas import tpu as pltpu
from jax.sharding import Mesh, PartitionSpec as P

HQ = 32
KVH = 4
DH = 128
ROWS = 64
SEQ = 8192
BLOCKS = 128
DOCS = 4
DOC_MOST = 4096
SLOTS = 8
HEADS = 4
LANES = HEADS * ROWS
TILE = 1024
TILES = (DOC_MOST + ROWS) // TILE + 2
RUN = 8
PIECE = RUN * ROWS

SCALE = 1.0 / math.sqrt(DH)
LOG2E = 1.0 / math.log(2.0)

AXES = ("yl", "c", "yh", "x", "z")
SIZES = (2, 2, 2, 4, 4)
YC = ("yh", "yl", "c")
Y = ("yh", "yl")


def stored_block(yl, c, yh, x, z):
    return (((yl * 2 + c) * 2 + yh) * 4 + x) * 4 + z


def block_rows(index):
    return pl.ds(pl.multiple_of(index * ROWS, ROWS), ROWS)


def attend_kernel(*refs):
    order_ref, seg_ref, qg_ref = refs[:3]
    pieces = refs[3:13]
    dq_ref, mine, other = refs[13], refs[14:16], refs[16:18]
    kv_ref, dk_acc, dv_acc, e_ref, qt_ref, gt_ref, q_ref, g_ref, dqt_ref = refs[18:]
    c, x, z = lax.axis_index("c"), lax.axis_index("x"), lax.axis_index("z")
    y = 2 * lax.axis_index("yh") + lax.axis_index("yl")

    def place_of(core, yh, far, i):
        near, yl = i // 2, i % 2
        sx, sz = (far, near) if yh == 0 else (near, far)
        sc = c if core == 0 else 1 - c
        return sc, yl, sx, sz

    def load(i, _):
        for core in range(2):
            for yh in range(2):
                for n in range(4):
                    sc, yl, sx, sz = place_of(core, yh, n, i)
                    sy = (y + 4 - 2 * yh - yl) % 4
                    place = order_ref[
                        stored_block(sy % 2, sc, sy // 2, (x + 4 - sx) % 4, (z + 4 - sz) % 4)
                    ]
                    source = pieces[yh * 4 + n] if core == 0 else pieces[8 + yh]
                    at = block_rows(i if core == 0 else n * RUN + i)
                    kv_ref[block_rows(place), :] = source[at, :]
        return 0

    lax.fori_loop(0, RUN, load, 0)

    kv_ref[SEQ:, :] = jnp.zeros((TILE, 2 * DH), jnp.bfloat16)
    dk_acc[...] = jnp.zeros_like(dk_acc)
    dv_acc[...] = jnp.zeros_like(dv_acc)
    seg = seg_ref[...]
    starts = [jnp.sum((seg < d).astype(jnp.int32)) for d in range(1, DOCS)]

    lane = lax.broadcasted_iota(jnp.int32, (1, LANES), 1)
    row_in_block = lane % ROWS
    tile_row = lax.broadcasted_iota(jnp.int32, (TILE, LANES), 0)

    def one_slot(s, _):
        place = order_ref[stored_block((s // 2) % 2, s % 2, s // 4, x, z)]
        first = place * ROWS
        lo = jnp.int32(0)
        lo_last = jnp.int32(0)
        row_pos = first + row_in_block
        row_lo = jnp.zeros((1, LANES), jnp.int32)
        for start in starts:
            lo = jnp.where(start <= first, start, lo)
            lo_last = jnp.where(start <= first + ROWS - 1, start, lo_last)
            row_lo = jnp.where(start <= row_pos, start, row_lo)
        base = lo // ROWS * ROWS
        length = first + ROWS - base
        count = (length + TILE // 2 - 1) // TILE
        ends = (length + TILE - 1) // TILE
        inner_lo = jnp.minimum((lo_last - base + TILE - 1) // TILE, count)
        inner_hi = jnp.maximum(jnp.minimum((first - base) // TILE, count), inner_lo)
        for h in range(HEADS):
            q_ref[h * ROWS:(h + 1) * ROWS, :] = qg_ref[s, :, h * DH:(h + 1) * DH]
            g_ref[h * ROWS:(h + 1) * ROWS, :] = qg_ref[s, :, (HEADS + h) * DH:(HEADS + h + 1) * DH]
        qt_ref[...] = q_ref[...].T
        gt_ref[...] = g_ref[...].T
        parts = qg_ref[s, :16, 2 * HEADS * DH:].astype(jnp.float32)
        delta = jnp.concatenate(
            [parts[i:i + 1] + parts[i + 2:i + 3] + parts[i + 4:i + 5] for i in range(2)], axis=1
        )

        def rows_of(t, size):
            return pl.ds(pl.multiple_of(base + t * TILE, ROWS), size)

        def kept(t, size):
            return pl.ds(pl.multiple_of(t * TILE, TILE), size)

        def scores(masked, size=TILE):
            def step(t, top):
                st = jnp.dot(
                    kv_ref[rows_of(t, size), :DH], qt_ref[...], preferred_element_type=jnp.float32
                )
                if masked:
                    pos = tile_row[:size] + (base + t * TILE)
                    st = jnp.where((pos <= row_pos) & (pos >= row_lo), st, -2e30)
                e_ref[kept(t, size), :] = st
                return jnp.maximum(top, jnp.max(st.reshape(size // 8, 8, LANES), axis=0))
            return step

        top = jnp.full((8, LANES), -1e30, jnp.float32)
        top = lax.fori_loop(0, inner_lo, scores(True), top)
        top = lax.fori_loop(inner_lo, inner_hi, scores(False), top)
        top = lax.fori_loop(inner_hi, count, scores(True), top)
        top = lax.fori_loop(count, ends, scores(True, TILE // 2), top)
        top = jnp.max(top, axis=0, keepdims=True) * (SCALE * LOG2E)

        def exps(size):
            def step(t, total):
                e = jnp.exp2(e_ref[kept(t, size), :] * (SCALE * LOG2E) - top)
                e_ref[kept(t, size), :] = e
                return total + jnp.sum(e.reshape(size // 8, 8, LANES), axis=0)
            return step

        total = lax.fori_loop(0, count, exps(TILE), jnp.zeros((8, LANES), jnp.float32))
        total = lax.fori_loop(count, ends, exps(TILE // 2), total)
        inverse = 1.0 / jnp.sum(total, axis=0, keepdims=True)
        dqt_ref[...] = jnp.zeros_like(dqt_ref)

        def grads(size):
            def step(t, _):
                p = e_ref[kept(t, size), :] * inverse
                dp = jnp.dot(kv_ref[rows_of(t, size), DH:], gt_ref[...], preferred_element_type=jnp.float32)
                pb = p.astype(jnp.bfloat16)
                ds = (p * (dp - delta) * SCALE).astype(jnp.bfloat16)
                dv_acc[rows_of(t, size), :] += jnp.dot(pb, g_ref[...], preferred_element_type=jnp.float32)
                dk_acc[rows_of(t, size), :] += jnp.dot(ds, q_ref[...], preferred_element_type=jnp.float32)
                dqt_ref[...] += lax.dot_general(
                    kv_ref[rows_of(t, size), :DH], ds, (((0,), (0,)), ((), ())),
                    preferred_element_type=jnp.float32,
                )
                return 0
            return step

        lax.fori_loop(0, count, grads(TILE), 0)
        lax.fori_loop(count, ends, grads(TILE // 2), 0)
        dq = dqt_ref[...].T.astype(jnp.bfloat16)
        for h in range(HEADS):
            dq_ref[s, :, h * DH:(h + 1) * DH] = dq[h * ROWS:(h + 1) * ROWS, :]
        return 0

    lax.fori_loop(0, SLOTS, one_slot, 0)

    def store(i, _):
        for core in range(2):
            for yh in range(2):
                for n in range(4):
                    sc, yl, sx, sz = place_of(core, yh, n, i)
                    place = order_ref[stored_block(yl, sc, yh, (x + sx) % 4, (z + sz) % 4)]
                    out = (mine if core == 0 else other)[yh]
                    dst = block_rows(n * RUN + i)
                    out[dst, :DH] = dk_acc[block_rows(place), :].astype(out.dtype)
                    out[dst, DH:] = dv_acc[block_rows(place), :].astype(out.dtype)
        return 0

    lax.fori_loop(0, RUN, store, 0)


def attend(order, seg, qg, pieces):
    vmem = pl.BlockSpec(memory_space=pltpu.VMEM)
    piece = (SEQ // 2 // 2, 2 * DH)
    result = pl.pallas_call(
        attend_kernel,
        out_shape=(
            jax.ShapeDtypeStruct((SLOTS, ROWS, HEADS * DH), jnp.bfloat16),
        )
        + (jax.ShapeDtypeStruct(piece, jnp.float32),) * 2
        + (jax.ShapeDtypeStruct(piece, jnp.bfloat16),) * 2,
        in_specs=[pl.BlockSpec(memory_space=pltpu.SMEM)] + [vmem] * 12,
        out_specs=(vmem,) * 5,
        scratch_shapes=[
            pltpu.VMEM((SEQ + TILE, 2 * DH), jnp.bfloat16),
            pltpu.VMEM((SEQ + TILE, DH), jnp.float32),
            pltpu.VMEM((SEQ + TILE, DH), jnp.float32),
            pltpu.VMEM((TILES * TILE, LANES), jnp.float32),
            pltpu.VMEM((DH, LANES), jnp.bfloat16),
            pltpu.VMEM((DH, LANES), jnp.bfloat16),
            pltpu.VMEM((LANES, DH), jnp.bfloat16),
            pltpu.VMEM((LANES, DH), jnp.bfloat16),
            pltpu.VMEM((DH, LANES), jnp.float32),
        ],
        compiler_params=pltpu.CompilerParams(vmem_limit_bytes=40 * 1024 * 1024),
        cost_estimate=pl.CostEstimate(
            flops=8 * 10**9, bytes_accessed=12 * 10**6, transcendentals=8 * 10**6
        ),
        name="attend",
    )(order, seg, qg, *pieces)
    return result[0], result[1:3], result[3:]


def exchange(value, axes):
    return lax.all_to_all(value, axes, split_axis=0, concat_axis=0, tiled=True)


def ahead(value, axis, n):
    return lax.ppermute(value, axis, [(i, (i + n) % 4) for i in range(4)])


def over_y(value, n):
    at = [place % 2 * 2 + place // 2 for place in range(4)]
    return lax.ppermute(value, ("yl", "yh"), [(at[i], at[(i + n) % 4]) for i in range(4)])


def other_core(value):
    return lax.ppermute(value, "c", [(0, 1), (1, 0)])


def added(terms):
    return sum(term.astype(jnp.float32) for term in terms)


def per_device(queries, keys, values, outputs, out_grads, block_order, segment_ids):
    kv = jnp.concatenate(
        [keys.reshape(ROWS, KVH, DH), values.reshape(ROWS, KVH, DH)], axis=-1
    ).transpose(1, 0, 2)
    y = lax.axis_index(Y)
    kv = [lax.dynamic_index_in_dim(kv, (y + n) % 4, 0, keepdims=False) for n in range(4)]
    kv = [kv[0]] + [over_y(kv[n], n) for n in (1, 2, 3)]
    ways = (("z", "x"), ("x", "z"))
    halves = [jnp.concatenate(kv[i:i + 2], axis=0) for i in (0, 2)]
    runs = [
        jnp.concatenate([half] + [ahead(half, way[0], n) for n in (1, 2, 3)], axis=0)
        for half, way in zip(halves, ways)
    ]
    products = outputs.astype(jnp.float32) * out_grads.astype(jnp.float32)
    delta = jnp.sum(products.reshape(ROWS, HQ, DH), axis=-1).T.reshape(SLOTS, 2, DH)
    high = lax.reduce_precision(delta, 8, 7)
    middle = lax.reduce_precision(delta - high, 8, 7)
    low = delta - high - middle
    parts = jnp.concatenate([high, middle, low], axis=1).astype(jnp.bfloat16)
    qg = jnp.concatenate(
        [
            queries.reshape(ROWS, SLOTS, HEADS * DH).transpose(1, 0, 2),
            out_grads.reshape(ROWS, SLOTS, HEADS * DH).transpose(1, 0, 2),
            jnp.pad(parts, ((0, 0), (0, ROWS - 6), (0, 0))),
        ],
        axis=-1,
    )
    runs = lax.optimization_barrier(runs)
    pieces = []
    for run, way in zip(runs, ways):
        pieces += [run] + [ahead(run, way[1], n) for n in (1, 2, 3)]

    qg = exchange(qg, YC)
    pieces, qg = lax.optimization_barrier((pieces, qg))
    pieces += [other_core(jnp.concatenate(pieces[i:i + 4], axis=0)) for i in (0, 4)]

    dq, mine, other = attend(block_order, segment_ids.reshape(SEQ // 128, 128), qg, pieces)

    back = (("x", "z"), ("z", "x"))
    came = [other_core(term) for term in other]
    both = []
    for own, term in zip(mine, came):
        half = (own + term.astype(jnp.float32)).astype(jnp.bfloat16)
        both += [half[i * PIECE:(i + 1) * PIECE] for i in range(4)]
    parts = []
    for yh, way in enumerate(back):
        own, *sent = both[yh * 4:yh * 4 + 4]
        terms = [own] + [ahead(term, way[0], n) for n, term in zip((1, 2, 3), sent)]
        parts.append(added(terms).astype(jnp.bfloat16).reshape(4, 2 * ROWS, 2 * DH))
    parts = lax.optimization_barrier(parts)
    sums = []
    for part, way in zip(parts, back):
        terms = [part[0]] + [ahead(part[n], way[1], n) for n in (1, 2, 3)]
        sums.append(added(terms).astype(jnp.bfloat16))
    sums = jnp.concatenate(sums, axis=0).reshape(KVH, ROWS, 2 * DH)
    sums = [lax.dynamic_index_in_dim(sums, (y + n) % 4, 0, keepdims=False) for n in range(4)]
    sums = jnp.stack([sums[0]] + [over_y(sums[n], n) for n in (1, 2, 3)])
    sums = [lax.dynamic_index_in_dim(sums, (y + 4 - g) % 4, 0, keepdims=False) for g in range(4)]
    sums = jnp.stack(sums).reshape(KVH, ROWS, 2, DH)
    grad_keys = sums[:, :, 0].transpose(1, 0, 2).reshape(ROWS, KVH * DH)
    grad_values = sums[:, :, 1].transpose(1, 0, 2).reshape(ROWS, KVH * DH)
    grad_queries = exchange(dq, YC).transpose(1, 0, 2).reshape(ROWS, HQ * DH)
    return grad_queries, grad_keys, grad_values


def solution(mesh):
    split = Mesh(mesh.devices.reshape(SIZES), AXES)
    rows = P(AXES, None)
    return jax.shard_map(
        per_device,
        mesh=split,
        in_specs=(rows, rows, rows, rows, rows, P(), P()),
        out_specs=(rows, rows, rows),
        check_vma=False,
    )
```

time: 166 us -> 131 us (0.79); the launches traced: 167 us -> 130 us
  waiting for transfers between devices: 53.9 us -> 31.5 us
  Pallas kernels: 38 us -> 21.8 us
  starting transfers between devices: 51 us -> 63.5 us
  local copies, waits for them, and re-layouts: 16.4 us -> 6.83 us
  other arithmetic: 6.85 us -> 5.09 us
    ppermute x24, waiting for transfers between devices: 45.4 us -> 22.3 us  [ahead(): return lax.ppermute(value, axis, [(i, (i + n) % 4) for i in range(4)])]
    pallas_call x1, Pallas kernels: 38 us -> 21.8 us  [attend(): pl.pallas_call(attend_kernel, out_shape=(jax.ShapeDtypeStruct((SLOTS, ROW...]
    ppermute x24, starting transfers between devices: 29.4 us -> 44.3 us  [ahead(): return lax.ppermute(value, axis, [(i, (i + n) % 4) for i in range(4)])]
    unnamed x57 -> x19, local copies, waits for them, and re-layouts: 12.9 us -> 1.52 us
    all_to_all x4 -> x2, starting transfers between devices: 18.2 us -> 8.3 us  [exchange(): return lax.all_to_all(value, axes, split_axis=0, concat_axis=0, tiled=True)]
    ppermute x0 -> x6, starting transfers between devices: none -> 9.72 us  [over_y(): lax.ppermute(value, ('yl', 'yh'), [(at[i], at[(i + n) % 4]) for i in rang...]
    all_to_all x4 -> x2, waiting for transfers between devices: 8.45 us -> 0.01 us  [exchange(): return lax.all_to_all(value, axes, split_axis=0, concat_axis=0, tiled=True)]
    ppermute x16 -> x4, waiting for transfers between devices: 0.04 us -> 5.65 us  [other_core(): return lax.ppermute(value, 'c', [(0, 1), (1, 0)])]
  transfers between devices with their start and end apart: 44 -> 36, of which waited for: 15 -> 14; matrix products, arithmetic and copies ran while one was open for 4% -> 6% of each run, Pallas kernels for 0% -> 0%
where the time goes in v1:
time: 131 us; the launch traced here: 130 us
  starting transfers between devices  63.5 us (48%)
  waiting for transfers between devices  31.5 us (24%)
  Pallas kernels  21.8 us (17%)
  local copies, waits for them, and re-layouts  6.83 us (5%)
  other arithmetic  5.09 us (4%)
    ppermute x24, starting transfers between devices, ahead(): return lax.ppermute(value, axis, [(i, (i + n) % 4) for i in range(4)])  44.3 us
    ppermute x24, waiting for transfers between devices, ahead(): return lax.ppermute(value, axis, [(i, (i + n) % 4) for i in range(4)])  22.3 us
    pallas_call x1, Pallas kernels, attend(): pl.pallas_call(attend_kernel, out_shape=(jax.ShapeDtypeStruct((SLOTS, ROW...  21.8 us
    ppermute x6, starting transfers between devices, over_y(): lax.ppermute(value, ('yl', 'yh'), [(at[i], at[(i + n) % 4]) for i in rang...  9.72 us
    all_to_all x2, starting transfers between devices, exchange(): return lax.all_to_all(value, axes, split_axis=0, concat_axis=0, tiled=True)  8.3 us
    ppermute x4, waiting for transfers between devices, other_core(): return lax.ppermute(value, 'c', [(0, 1), (1, 0)])  5.65 us
    ppermute x6, waiting for transfers between devices, over_y(): lax.ppermute(value, ('yl', 'yh'), [(at[i], at[(i + n) % 4]) for i in rang...  3.48 us
  transfers between devices with their start and end apart: 36, of which 14 were waited for; matrix products, arithmetic and copies ran while one was open for 6% of the time, Pallas kernels for 0%

profile of v1, /device:TPU:0, one launch (start us, length us, event | category | flops | bytes accessed | tf_op | source)
XLA Modules:
  0.0 129.8 jit_solution(4123791146000270395)
XLA Ops:
  0.7 0.8 copy-done
  1.5 0.9 bitcast_dynamic-update-slice_fusion
  2.4 3.2 %collective-permute-start.5 = (bf16[64,256]{1,0:T(8,128)(2,1)S(1)}, bf16[64,256]{1,0:T(8,128)(2,1)S(1)}, u32[]{:S(2)}, u32[]{:S(2)}) collective-permute-start(bf16[64,256]{1,0:T(8,128)(2,1)S(1)} %get-tuple-element.63), channel_id=1, source_target_pairs={{0,80},{64,0},{16,64},{80,16},{1,81},{65,1},{17,65},{81,17},{2,82}... | collective-permute-start | bytes 98312 | tf_op jit(solution)/shard_map/ppermute | solution.py:228
  6.2 1.0 collective-permute-start
  7.2 1.3 %multiply_bitcast_fusion = f32[8,8,32,128]{3,1,2,0:T(8,128)S(1)} fusion(bf16[64,4096]{1,0:T(8,128)(2,1)} %param.11, bf16[64,4096]{1,0:T(8,128)(2,1)} %param.10), kind=kLoop, calls=%fused_computation.5 | loop fusion | flops 786432 | bytes 2097152
  9.8 1.2 pad_maximum_fusion
  11.1 3.6 %all-to-all-start = ((bf16[8,64,1152]{2,1,0:T(8,128)(2,1)}), bf16[8,64,1152]{2,1,0:T(8,128)(2,1)S(1)}, u32[]{:S(2)}, u32[]{:S(2)}) async-start(bf16[8,64,1152]{2,1,0:T(8,128)(2,1)} %pad_maximum_fusion), calls=%async_computation | async-start | bytes 2359296 | tf_op jit(solution)/shard_map/all_to_all | solution.py:219
  14.7 4.1 %collective-permute-start.3 = (bf16[128,256]{1,0:T(8,128)(2,1)S(1)}, bf16[128,256]{1,0:T(8,128)(2,1)S(1)}, u32[]{:S(2)}, u32[]{:S(2)}) collective-permute-start(bf16[128,256]{1,0:T(8,128)(2,1)S(1)} %pad_maximum_fusion.6), channel_id=1, source_target_pairs={{0,3},{1,0},{2,1},{3,2},{4,7},{5,4},{6,5},{7,6},{8,11},{9,8},{10,9... | collective-permute-start | bytes 196616 | tf_op jit(solution)/shard_map/ppermute | solution.py:223
  18.8 1.3 collective-permute-start.1
  20.1 2.8 %collective-permute-start.8 = (bf16[128,256]{1,0:T(8,128)(2,1)S(1)}, bf16[128,256]{1,0:T(8,128)(2,1)S(1)}, u32[]{:S(2)}, u32[]{:S(2)}) collective-permute-start(bf16[128,256]{1,0:T(8,128)(2,1)S(1)} %get-tuple-element.66), channel_id=1, source_target_pairs={{0,12},{4,0},{8,4},{12,8},{1,13},{5,1},{9,5},{13,9},{2,14},{6,2},{... | collective-permute-start | bytes 196616 | tf_op jit(solution)/shard_map/ppermute | solution.py:223
  22.9 0.8 collective-permute-start.7
  23.7 1.9 %collective-permute-done.1 = bf16[128,256]{1,0:T(8,128)(2,1)S(1)} collective-permute-done((bf16[128,256]{1,0:T(8,128)(2,1)S(1)}, bf16[128,256]{1,0:T(8,128)(2,1)S(1)}, u32[]{:S(2)}, u32[]{:S(2)}) %collective-permute-start.1) | collective-permute-done | bytes 65568 | tf_op jit(solution)/shard_map/ppermute | solution.py:223
  25.6 1.5 %collective-permute-start.6 = (bf16[128,256]{1,0:T(8,128)(2,1)S(1)}, bf16[128,256]{1,0:T(8,128)(2,1)S(1)}, u32[]{:S(2)}, u32[]{:S(2)}) collective-permute-start(bf16[128,256]{1,0:T(8,128)(2,1)S(1)} %get-tuple-element.66), channel_id=1, source_target_pairs={{0,4},{4,8},{8,12},{12,0},{1,5},{5,9},{9,13},{13,1},{2,6},{6,10},{... | collective-permute-start | bytes 196616 | tf_op jit(solution)/shard_map/ppermute | solution.py:223
  27.1 3.9 %collective-permute-done.6 = bf16[128,256]{1,0:T(8,128)(2,1)S(1)} collective-permute-done((bf16[128,256]{1,0:T(8,128)(2,1)S(1)}, bf16[128,256]{1,0:T(8,128)(2,1)S(1)}, u32[]{:S(2)}, u32[]{:S(2)}) %collective-permute-start.6) | collective-permute-done | bytes 65568 | tf_op jit(solution)/shard_map/ppermute | solution.py:223
  31.1 1.6 %collective-permute-start.11 = (bf16[512,256]{1,0:T(8,128)(2,1)S(1)}, bf16[512,256]{1,0:T(8,128)(2,1)S(1)}, u32[]{:S(2)}, u32[]{:S(2)}) collective-permute-start(bf16[512,256]{1,0:T(8,128)(2,1)S(1)} %constant_dynamic-update-slice_fusion.refs_3_), channel_id=1, source_target_pairs={{0,12},{4,0},{8,4},{12,8},{1,13},{5,1},{9,5},{13,9},{2,14},{6,2},{... | collective-permute-start | bytes 786440 | tf_op jit(solution)/shard_map/ppermute | solution.py:223
  32.8 0.8 collective-permute-start.10
  33.6 0.9 collective-permute-start.9
  34.4 0.9 collective-permute-start.14
  35.3 1.3 collective-permute-start.13
  36.6 3.9 %collective-permute-done.11.refs_6_ = bf16[512,256]{1,0:T(8,128)(2,1)S(1)} collective-permute-done((bf16[512,256]{1,0:T(8,128)(2,1)S(1)}, bf16[512,256]{1,0:T(8,128)(2,1)S(1)}, u32[]{:S(2)}, u32[]{:S(2)}) %collective-permute-start.11) | collective-permute-done | bytes 262176 | tf_op jit(solution)/shard_map/ppermute | solution.py:223
  41.0 2.5 %collective-permute-done.10.refs_5_ = bf16[512,256]{1,0:T(8,128)(2,1)S(1)} collective-permute-done((bf16[512,256]{1,0:T(8,128)(2,1)S(1)}, bf16[512,256]{1,0:T(8,128)(2,1)S(1)}, u32[]{:S(2)}, u32[]{:S(2)}) %collective-permute-start.10) | collective-permute-done | bytes 262176 | tf_op jit(solution)/shard_map/ppermute | solution.py:223
  43.5 2.9 %collective-permute-done.9.refs_4_ = bf16[512,256]{1,0:T(8,128)(2,1)S(1)} collective-permute-done((bf16[512,256]{1,0:T(8,128)(2,1)S(1)}, bf16[512,256]{1,0:T(8,128)(2,1)S(1)}, u32[]{:S(2)}, u32[]{:S(2)}) %collective-permute-start.9) | collective-permute-done | bytes 262176 | tf_op jit(solution)/shard_map/ppermute | solution.py:223
  46.4 2.1 %collective-permute-done.12.refs_8_ = bf16[512,256]{1,0:T(8,128)(2,1)S(1)} collective-permute-done((bf16[512,256]{1,0:T(8,128)(2,1)S(1)}, bf16[512,256]{1,0:T(8,128)(2,1)S(1)}, u32[]{:S(2)}, u32[]{:S(2)}) %collective-permute-start.12) | collective-permute-done | bytes 262176 | tf_op jit(solution)/shard_map/ppermute | solution.py:223
  49.4 2.0 %collective-permute-done.16.refs_12_ = bf16[2048,256]{1,0:T(8,128)(2,1)S(1)} collective-permute-done((bf16[2048,256]{1,0:T(8,128)(2,1)S(1)}, bf16[2048,256]{1,0:T(8,128)(2,1)S(1)}, u32[]{:S(2)}, u32[]{:S(2)}) %collective-permute-start.16) | collective-permute-done | bytes 1048608 | tf_op jit(solution)/shard_map/ppermute | solution.py:232
  51.4 1.5 %collective-permute-done.15.refs_11_ = bf16[2048,256]{1,0:T(8,128)(2,1)S(1)} collective-permute-done((bf16[2048,256]{1,0:T(8,128)(2,1)S(1)}, bf16[2048,256]{1,0:T(8,128)(2,1)S(1)}, u32[]{:S(2)}, u32[]{:S(2)}) %collective-permute-start.15) | collective-permute-done | bytes 1048608 | tf_op jit(solution)/shard_map/ppermute | solution.py:232
  52.9 21.8 %attend.1 = (bf16[8,64,512]{2,1,0:T(8,128)(2,1)}, f32[2048,256]{1,0:T(8,128)S(1)}, f32[2048,256]{1,0:T(8,128)S(1)}, bf16[2048,256]{1,0:T(8,128)(2,1)S(1)}, bf16[2048,256]{1,0:T(8,128)(2,1)S(1)}) custom-call(s32[128]{0:T(128)S(1)} %copy-done.2, s32[64,128]{1,0:T(8,128)S(1)} %bitcast.83, bf16[8,64,1152]{2,1,0:T(8,128)(2,1)S(1)} %all-to-all-done.refs_2_, ...), custom_call_target="tpu_custom_call" | custom-call | flops 8000000000 | bytes 12000000 | tf_op jit(solution)/shard_map/attend/pallas_call | solution.py:189
  75.2 2.1 %collective-permute-done.17 = bf16[2048,256]{1,0:T(8,128)(2,1)S(1)} collective-permute-done((bf16[2048,256]{1,0:T(8,128)(2,1)S(1)}, bf16[2048,256]{1,0:T(8,128)(2,1)S(1)}, u32[]{:S(2)}, u32[]{:S(2)}) %collective-permute-start.17) | collective-permute-done | bytes 1048608 | tf_op jit(solution)/shard_map/ppermute | solution.py:232
  77.6 0.8 fusion.13
  78.5 3.2 %collective-permute-start.20 = (bf16[512,256]{1,0:T(8,128)(2,1)}, bf16[512,256]{1,0:T(8,128)(2,1)S(1)}, u32[]{:S(2)}, u32[]{:S(2)}) collective-permute-start(bf16[512,256]{1,0:T(8,128)(2,1)} %get-tuple-element.45), channel_id=1, source_target_pairs={{0,12},{4,0},{8,4},{12,8},{1,13},{5,1},{9,5},{13,9},{2,14},{6,2},{... | collective-permute-start | bytes 786440 | tf_op jit(solution)/shard_map/ppermute | solution.py:223
  82.1 0.9 fusion.12
  83.0 6.2 %collective-permute-start.22 = (bf16[512,256]{1,0:T(8,128)(2,1)}, bf16[512,256]{1,0:T(8,128)(2,1)}, u32[]{:S(2)}, u32[]{:S(2)}) collective-permute-start(bf16[512,256]{1,0:T(8,128)(2,1)} %get-tuple-element.41), channel_id=1, source_target_pairs={{0,1},{1,2},{2,3},{3,0},{4,5},{5,6},{6,7},{7,4},{8,9},{9,10},{10,1... | collective-permute-start | bytes 786440 | tf_op jit(solution)/shard_map/ppermute | solution.py:223
  89.2 7.9 %collective-permute-start.23 = (bf16[512,256]{1,0:T(8,128)(2,1)}, bf16[512,256]{1,0:T(8,128)(2,1)}, u32[]{:S(2)}, u32[]{:S(2)}) collective-permute-start(bf16[512,256]{1,0:T(8,128)(2,1)} %get-tuple-element.43), channel_id=1, source_target_pairs={{0,2},{1,3},{2,0},{3,1},{4,6},{5,7},{6,4},{7,5},{8,10},{9,11},{10,... | collective-permute-start | bytes 786440 | tf_op jit(solution)/shard_map/ppermute | solution.py:223
  97.1 4.7 %all-to-all-start.1 = ((bf16[8,64,512]{2,1,0:T(8,128)(2,1)}), bf16[8,64,512]{2,1,0:T(8,128)(2,1)S(1)}, u32[]{:S(2)}, u32[]{:S(2)}) async-start(bf16[8,64,512]{2,1,0:T(8,128)(2,1)} %get-tuple-element.32), calls=%async_computation.1 | async-start | bytes 1048576 | tf_op jit(solution)/shard_map/all_to_all | solution.py:219
  102.0 1.2 collective-permute-done.23
  103.2 1.2 add_convert_fusion.2
  104.5 3.2 %collective-permute-start.27 = (bf16[128,256]{1,0:T(8,128)(2,1)S(1)}, bf16[128,256]{1,0:T(8,128)(2,1)S(1)}, u32[]{:S(2)}, u32[]{:S(2)}) collective-permute-start(bf16[128,256]{1,0:T(8,128)(2,1)S(1)} %get-tuple-element.48), channel_id=1, source_target_pairs={{0,3},{1,0},{2,1},{3,2},{4,7},{5,4},{6,5},{7,6},{8,11},{9,8},{10,9... | collective-permute-start | bytes 196616 | tf_op jit(solution)/shard_map/ppermute | solution.py:223
  107.7 2.0 %collective-permute-start.26 = (bf16[128,256]{1,0:T(8,128)(2,1)S(1)}, bf16[128,256]{1,0:T(8,128)(2,1)S(1)}, u32[]{:S(2)}, u32[]{:S(2)}) collective-permute-start(bf16[128,256]{1,0:T(8,128)(2,1)S(1)} %get-tuple-element.49), channel_id=1, source_target_pairs={{0,2},{1,3},{2,0},{3,1},{4,6},{5,7},{6,4},{7,5},{8,10},{9,11},{10,... | collective-permute-start | bytes 196616 | tf_op jit(solution)/shard_map/ppermute | solution.py:223
  110.4 2.7 %collective-permute-start.30 = (bf16[128,256]{1,0:T(8,128)(2,1)S(1)}, bf16[128,256]{1,0:T(8,128)(2,1)S(1)}, u32[]{:S(2)}, u32[]{:S(2)}) collective-permute-start(bf16[128,256]{1,0:T(8,128)(2,1)S(1)} %get-tuple-element.51), channel_id=1, source_target_pairs={{0,12},{4,0},{8,4},{12,8},{1,13},{5,1},{9,5},{13,9},{2,14},{6,2},{... | collective-permute-start | bytes 196616 | tf_op jit(solution)/shard_map/ppermute | solution.py:223
  113.1 1.8 %collective-permute-start.29 = (bf16[128,256]{1,0:T(8,128)(2,1)S(1)}, bf16[128,256]{1,0:T(8,128)(2,1)S(1)}, u32[]{:S(2)}, u32[]{:S(2)}) collective-permute-start(bf16[128,256]{1,0:T(8,128)(2,1)S(1)} %get-tuple-element.52), channel_id=1, source_target_pairs={{0,8},{4,12},{8,0},{12,4},{1,9},{5,13},{9,1},{13,5},{2,10},{6,14},... | collective-permute-start | bytes 196616 | tf_op jit(solution)/shard_map/ppermute | solution.py:223
  115.0 0.7 collective-permute-done.28
  115.7 3.2 %collective-permute-done.29 = bf16[128,256]{1,0:T(8,128)(2,1)S(1)} collective-permute-done((bf16[128,256]{1,0:T(8,128)(2,1)S(1)}, bf16[128,256]{1,0:T(8,128)(2,1)S(1)}, u32[]{:S(2)}, u32[]{:S(2)}) %collective-permute-start.29) | collective-permute-done | bytes 65568 | tf_op jit(solution)/shard_map/ppermute | solution.py:223
  119.0 3.3 %collective-permute-start.33 = (bf16[64,256]{1,0:T(8,128)(2,1)S(1)}, bf16[64,256]{1,0:T(8,128)(2,1)S(1)}, u32[]{:S(2)}, u32[]{:S(2)}) collective-permute-start(bf16[64,256]{1,0:T(8,128)(2,1)S(1)} %get-tuple-element.60), channel_id=1, source_target_pairs={{0,80},{64,0},{16,64},{80,16},{1,81},{65,1},{17,65},{81,17},{2,82}... | collective-permute-start | bytes 98312 | tf_op jit(solution)/shard_map/ppermute | solution.py:228
  122.3 0.9 collective-permute-start.32
  123.1 0.8 collective-permute-start.31
  123.9 0.8 copy.46
  124.8 2.9 %collective-permute-done.32 = bf16[64,256]{1,0:T(8,128)(2,1)S(1)} collective-permute-done((bf16[64,256]{1,0:T(8,128)(2,1)S(1)}, bf16[64,256]{1,0:T(8,128)(2,1)S(1)}, u32[]{:S(2)}, u32[]{:S(2)}) %collective-permute-start.32) | collective-permute-done | bytes 32800 | tf_op jit(solution)/shard_map/ppermute | solution.py:228
  128.6 0.6 copy_bitcast_fusion
  129.2 0.6 copy_bitcast_fusion.1
  (80 shorter events, 6.4 us)
Async XLA Ops:
  0.6 0.8 copy-start
  2.4 17.7 %collective-permute-start.5 = (bf16[64,256]{1,0:T(8,128)(2,1)S(1)}, bf16[64,256]{1,0:T(8,128)(2,1)S(1)}, u32[]{:S(2)}, u32[]{:S(2)}) collective-permute-start(bf16[64,256]{1,0:T(8,128)(2,1)S(1)} %get-tuple-element.63), channel_id=1, source_target_pairs={{0,80},{64,0},{16,64},{80,16},{1,81},{65,1},{17,65},{81,17},{2,82}... | collective-permute-start | bytes 98312 | tf_op jit(solution)/shard_map/ppermute | solution.py:228
  5.6 14.5 %collective-permute-start.4 = (bf16[64,256]{1,0:T(8,128)(2,1)S(1)}, bf16[64,256]{1,0:T(8,128)(2,1)S(1)}, u32[]{:S(2)}, u32[]{:S(2)}) collective-permute-start(bf16[64,256]{1,0:T(8,128)(2,1)S(1)} %get-tuple-element.64), channel_id=1, source_target_pairs={{0,16},{64,80},{16,0},{80,64},{1,17},{65,81},{17,1},{81,65},{2,18}... | collective-permute-start | bytes 98312 | tf_op jit(solution)/shard_map/ppermute | solution.py:228
  6.2 8.5 %collective-permute-start = (bf16[64,256]{1,0:T(8,128)(2,1)S(1)}, bf16[64,256]{1,0:T(8,128)(2,1)S(1)}, u32[]{:S(2)}, u32[]{:S(2)}) collective-permute-start(bf16[64,256]{1,0:T(8,128)(2,1)S(1)} %get-tuple-element.65), channel_id=1, source_target_pairs={{0,64},{64,16},{16,80},{80,0},{1,65},{65,17},{17,81},{81,1},{2,66}... | collective-permute-start | bytes 98312 | tf_op jit(solution)/shard_map/ppermute | solution.py:228
  8.5 1.0 copy-start.3
  8.5 1.2 copy-start.4
  11.1 37.5 %all-to-all-start = ((bf16[8,64,1152]{2,1,0:T(8,128)(2,1)}), bf16[8,64,1152]{2,1,0:T(8,128)(2,1)S(1)}, u32[]{:S(2)}, u32[]{:S(2)}) async-start(bf16[8,64,1152]{2,1,0:T(8,128)(2,1)} %pad_maximum_fusion), calls=%async_computation | async-start | bytes 2359296 | tf_op jit(solution)/shard_map/all_to_all | solution.py:219
  14.7 12.4 %collective-permute-start.3 = (bf16[128,256]{1,0:T(8,128)(2,1)S(1)}, bf16[128,256]{1,0:T(8,128)(2,1)S(1)}, u32[]{:S(2)}, u32[]{:S(2)}) collective-permute-start(bf16[128,256]{1,0:T(8,128)(2,1)S(1)} %pad_maximum_fusion.6), channel_id=1, source_target_pairs={{0,3},{1,0},{2,1},{3,2},{4,7},{5,4},{6,5},{7,6},{8,11},{9,8},{10,9... | collective-permute-start | bytes 196616 | tf_op jit(solution)/shard_map/ppermute | solution.py:223
  18.8 8.3 %collective-permute-start.2 = (bf16[128,256]{1,0:T(8,128)(2,1)S(1)}, bf16[128,256]{1,0:T(8,128)(2,1)S(1)}, u32[]{:S(2)}, u32[]{:S(2)}) collective-permute-start(bf16[128,256]{1,0:T(8,128)(2,1)S(1)} %pad_maximum_fusion.6), channel_id=1, source_target_pairs={{0,2},{1,3},{2,0},{3,1},{4,6},{5,7},{6,4},{7,5},{8,10},{9,11},{10,... | collective-permute-start | bytes 196616 | tf_op jit(solution)/shard_map/ppermute | solution.py:223
  18.8 6.8 %collective-permute-start.1 = (bf16[128,256]{1,0:T(8,128)(2,1)S(1)}, bf16[128,256]{1,0:T(8,128)(2,1)S(1)}, u32[]{:S(2)}, u32[]{:S(2)}) collective-permute-start(bf16[128,256]{1,0:T(8,128)(2,1)S(1)} %pad_maximum_fusion.6), channel_id=1, source_target_pairs={{0,1},{1,2},{2,3},{3,0},{4,5},{5,6},{6,7},{7,4},{8,9},{9,10},{10,1... | collective-permute-start | bytes 196616 | tf_op jit(solution)/shard_map/ppermute | solution.py:223
  20.1 11.0 %collective-permute-start.8 = (bf16[128,256]{1,0:T(8,128)(2,1)S(1)}, bf16[128,256]{1,0:T(8,128)(2,1)S(1)}, u32[]{:S(2)}, u32[]{:S(2)}) collective-permute-start(bf16[128,256]{1,0:T(8,128)(2,1)S(1)} %get-tuple-element.66), channel_id=1, source_target_pairs={{0,12},{4,0},{8,4},{12,8},{1,13},{5,1},{9,5},{13,9},{2,14},{6,2},{... | collective-permute-start | bytes 196616 | tf_op jit(solution)/shard_map/ppermute | solution.py:223
  22.9 8.1 %collective-permute-start.7 = (bf16[128,256]{1,0:T(8,128)(2,1)S(1)}, bf16[128,256]{1,0:T(8,128)(2,1)S(1)}, u32[]{:S(2)}, u32[]{:S(2)}) collective-permute-start(bf16[128,256]{1,0:T(8,128)(2,1)S(1)} %get-tuple-element.66), channel_id=1, source_target_pairs={{0,8},{4,12},{8,0},{12,4},{1,9},{5,13},{9,1},{13,5},{2,10},{6,14},... | collective-permute-start | bytes 196616 | tf_op jit(solution)/shard_map/ppermute | solution.py:223
  25.6 5.5 %collective-permute-start.6 = (bf16[128,256]{1,0:T(8,128)(2,1)S(1)}, bf16[128,256]{1,0:T(8,128)(2,1)S(1)}, u32[]{:S(2)}, u32[]{:S(2)}) collective-permute-start(bf16[128,256]{1,0:T(8,128)(2,1)S(1)} %get-tuple-element.66), channel_id=1, source_target_pairs={{0,4},{4,8},{8,12},{12,0},{1,5},{5,9},{9,13},{13,1},{2,6},{6,10},{... | collective-permute-start | bytes 196616 | tf_op jit(solution)/shard_map/ppermute | solution.py:223
  31.1 21.7 %copy-start.1 = (s32[8192]{0:T(1024)S(1)}, s32[8192]{0:T(1024)}, u32[]{:S(2)}) copy-start(s32[8192]{0:T(1024)} %param.13) | copy-start | bytes 98308
  31.1 21.7 %copy-start.2 = (s32[128]{0:T(128)S(1)}, s32[128]{0:T(128)}, u32[]{:S(2)}) copy-start(s32[128]{0:T(128)} %refs_0_.1) | copy-start | bytes 1540
  31.1 9.3 %collective-permute-start.11 = (bf16[512,256]{1,0:T(8,128)(2,1)S(1)}, bf16[512,256]{1,0:T(8,128)(2,1)S(1)}, u32[]{:S(2)}, u32[]{:S(2)}) collective-permute-start(bf16[512,256]{1,0:T(8,128)(2,1)S(1)} %constant_dynamic-update-slice_fusion.refs_3_), channel_id=1, source_target_pairs={{0,12},{4,0},{8,4},{12,8},{1,13},{5,1},{9,5},{13,9},{2,14},{6,2},{... | collective-permute-start | bytes 786440 | tf_op jit(solution)/shard_map/ppermute | solution.py:223
  32.8 10.7 %collective-permute-start.10 = (bf16[512,256]{1,0:T(8,128)(2,1)S(1)}, bf16[512,256]{1,0:T(8,128)(2,1)S(1)}, u32[]{:S(2)}, u32[]{:S(2)}) collective-permute-start(bf16[512,256]{1,0:T(8,128)(2,1)S(1)} %constant_dynamic-update-slice_fusion.refs_3_), channel_id=1, source_target_pairs={{0,8},{4,12},{8,0},{12,4},{1,9},{5,13},{9,1},{13,5},{2,10},{6,14},... | collective-permute-start | bytes 786440 | tf_op jit(solution)/shard_map/ppermute | solution.py:223
  33.6 12.9 %collective-permute-start.9 = (bf16[512,256]{1,0:T(8,128)(2,1)S(1)}, bf16[512,256]{1,0:T(8,128)(2,1)S(1)}, u32[]{:S(2)}, u32[]{:S(2)}) collective-permute-start(bf16[512,256]{1,0:T(8,128)(2,1)S(1)} %constant_dynamic-update-slice_fusion.refs_3_), channel_id=1, source_target_pairs={{0,4},{4,8},{8,12},{12,0},{1,5},{5,9},{9,13},{13,1},{2,6},{6,10},{... | collective-permute-start | bytes 786440 | tf_op jit(solution)/shard_map/ppermute | solution.py:223
  34.4 12.0 %collective-permute-start.14 = (bf16[512,256]{1,0:T(8,128)(2,1)S(1)}, bf16[512,256]{1,0:T(8,128)(2,1)S(1)}, u32[]{:S(2)}, u32[]{:S(2)}) collective-permute-start(bf16[512,256]{1,0:T(8,128)(2,1)S(1)} %constant_dynamic-update-slice_fusion.7.refs_7_), channel_id=1, source_target_pairs={{0,3},{1,0},{2,1},{3,2},{4,7},{5,4},{6,5},{7,6},{8,11},{9,8},{10,9... | collective-permute-start | bytes 786440 | tf_op jit(solution)/shard_map/ppermute | solution.py:223
  35.3 11.1 %collective-permute-start.13 = (bf16[512,256]{1,0:T(8,128)(2,1)S(1)}, bf16[512,256]{1,0:T(8,128)(2,1)S(1)}, u32[]{:S(2)}, u32[]{:S(2)}) collective-permute-start(bf16[512,256]{1,0:T(8,128)(2,1)S(1)} %constant_dynamic-update-slice_fusion.7.refs_7_), channel_id=1, source_target_pairs={{0,2},{1,3},{2,0},{3,1},{4,6},{5,7},{6,4},{7,5},{8,10},{9,11},{10,... | collective-permute-start | bytes 786440 | tf_op jit(solution)/shard_map/ppermute | solution.py:223
  40.5 8.1 %collective-permute-start.12 = (bf16[512,256]{1,0:T(8,128)(2,1)S(1)}, bf16[512,256]{1,0:T(8,128)(2,1)S(1)}, u32[]{:S(2)}, u32[]{:S(2)}) collective-permute-start(bf16[512,256]{1,0:T(8,128)(2,1)S(1)} %constant_dynamic-update-slice_fusion.7.refs_7_), channel_id=1, source_target_pairs={{0,1},{1,2},{2,3},{3,0},{4,5},{5,6},{6,7},{7,4},{8,9},{9,10},{10,1... | collective-permute-start | bytes 786440 | tf_op jit(solution)/shard_map/ppermute | solution.py:223
  48.6 2.7 %collective-permute-start.16 = (bf16[2048,256]{1,0:T(8,128)(2,1)S(1)}, bf16[2048,256]{1,0:T(8,128)(2,1)S(1)}, u32[]{:S(2)}, u32[]{:S(2)}) collective-permute-start(bf16[2048,256]{1,0:T(8,128)(2,1)S(1)} %pad_maximum_fusion.2), channel_id=1, source_target_pairs={{0,32},{32,0},{1,33},{33,1},{2,34},{34,2},{3,35},{35,3},{4,36},{36... | collective-permute-start | bytes 3145736 | tf_op jit(solution)/shard_map/ppermute | solution.py:232
  48.8 4.1 %collective-permute-start.15 = (bf16[2048,256]{1,0:T(8,128)(2,1)S(1)}, bf16[2048,256]{1,0:T(8,128)(2,1)S(1)}, u32[]{:S(2)}, u32[]{:S(2)}) collective-permute-start(bf16[2048,256]{1,0:T(8,128)(2,1)S(1)} %pad_maximum_fusion.1), channel_id=1, source_target_pairs={{0,32},{32,0},{1,33},{33,1},{2,34},{34,2},{3,35},{35,3},{4,36},{36... | collective-permute-start | bytes 3145736 | tf_op jit(solution)/shard_map/ppermute | solution.py:232
  74.7 2.7 %collective-permute-start.17 = (bf16[2048,256]{1,0:T(8,128)(2,1)S(1)}, bf16[2048,256]{1,0:T(8,128)(2,1)S(1)}, u32[]{:S(2)}, u32[]{:S(2)}) collective-permute-start(bf16[2048,256]{1,0:T(8,128)(2,1)S(1)} %get-tuple-element.34), channel_id=1, source_target_pairs={{0,32},{32,0},{1,33},{33,1},{2,34},{34,2},{3,35},{35,3},{4,36},{36... | collective-permute-start | bytes 3145736 | tf_op jit(solution)/shard_map/ppermute | solution.py:232
  74.8 7.1 %collective-permute-start.21 = (bf16[2048,256]{1,0:T(8,128)(2,1)S(1)}, bf16[2048,256]{1,0:T(8,128)(2,1)S(1)}, u32[]{:S(2)}, u32[]{:S(2)}) collective-permute-start(bf16[2048,256]{1,0:T(8,128)(2,1)S(1)} %get-tuple-element.36), channel_id=1, source_target_pairs={{0,32},{32,0},{1,33},{33,1},{2,34},{34,2},{3,35},{35,3},{4,36},{36... | collective-permute-start | bytes 3145736 | tf_op jit(solution)/shard_map/ppermute | solution.py:232
  78.5 10.8 %collective-permute-start.18 = (bf16[512,256]{1,0:T(8,128)(2,1)S(1)}, bf16[512,256]{1,0:T(8,128)(2,1)S(1)}, u32[]{:S(2)}, u32[]{:S(2)}) collective-permute-start(bf16[512,256]{1,0:T(8,128)(2,1)S(1)} %get-tuple-element.44), channel_id=1, source_target_pairs={{0,4},{4,8},{8,12},{12,0},{1,5},{5,9},{9,13},{13,1},{2,6},{6,10},{... | collective-permute-start | bytes 786440 | tf_op jit(solution)/shard_map/ppermute | solution.py:223
  78.5 23.4 %collective-permute-start.20 = (bf16[512,256]{1,0:T(8,128)(2,1)}, bf16[512,256]{1,0:T(8,128)(2,1)S(1)}, u32[]{:S(2)}, u32[]{:S(2)}) collective-permute-start(bf16[512,256]{1,0:T(8,128)(2,1)} %get-tuple-element.45), channel_id=1, source_target_pairs={{0,12},{4,0},{8,4},{12,8},{1,13},{5,1},{9,5},{13,9},{2,14},{6,2},{... | collective-permute-start | bytes 786440 | tf_op jit(solution)/shard_map/ppermute | solution.py:223
  81.7 20.1 %collective-permute-start.19 = (bf16[512,256]{1,0:T(8,128)(2,1)}, bf16[512,256]{1,0:T(8,128)(2,1)S(1)}, u32[]{:S(2)}, u32[]{:S(2)}) collective-permute-start(bf16[512,256]{1,0:T(8,128)(2,1)} %get-tuple-element.46), channel_id=1, source_target_pairs={{0,8},{4,12},{8,0},{12,4},{1,9},{5,13},{9,1},{13,5},{2,10},{6,14},... | collective-permute-start | bytes 786440 | tf_op jit(solution)/shard_map/ppermute | solution.py:223
  83.0 18.9 %collective-permute-start.22 = (bf16[512,256]{1,0:T(8,128)(2,1)}, bf16[512,256]{1,0:T(8,128)(2,1)}, u32[]{:S(2)}, u32[]{:S(2)}) collective-permute-start(bf16[512,256]{1,0:T(8,128)(2,1)} %get-tuple-element.41), channel_id=1, source_target_pairs={{0,1},{1,2},{2,3},{3,0},{4,5},{5,6},{6,7},{7,4},{8,9},{9,10},{10,1... | collective-permute-start | bytes 786440 | tf_op jit(solution)/shard_map/ppermute | solution.py:223
  89.2 12.8 %collective-permute-start.24 = (bf16[512,256]{1,0:T(8,128)(2,1)}, bf16[512,256]{1,0:T(8,128)(2,1)}, u32[]{:S(2)}, u32[]{:S(2)}) collective-permute-start(bf16[512,256]{1,0:T(8,128)(2,1)} %get-tuple-element.42), channel_id=1, source_target_pairs={{0,3},{1,0},{2,1},{3,2},{4,7},{5,4},{6,5},{7,6},{8,11},{9,8},{10,9... | collective-permute-start | bytes 786440 | tf_op jit(solution)/shard_map/ppermute | solution.py:223
  89.2 14.0 %collective-permute-start.23 = (bf16[512,256]{1,0:T(8,128)(2,1)}, bf16[512,256]{1,0:T(8,128)(2,1)}, u32[]{:S(2)}, u32[]{:S(2)}) collective-permute-start(bf16[512,256]{1,0:T(8,128)(2,1)} %get-tuple-element.43), channel_id=1, source_target_pairs={{0,2},{1,3},{2,0},{3,1},{4,6},{5,7},{6,4},{7,5},{8,10},{9,11},{10,... | collective-permute-start | bytes 786440 | tf_op jit(solution)/shard_map/ppermute | solution.py:223
  97.1 26.8 %all-to-all-start.1 = ((bf16[8,64,512]{2,1,0:T(8,128)(2,1)}), bf16[8,64,512]{2,1,0:T(8,128)(2,1)S(1)}, u32[]{:S(2)}, u32[]{:S(2)}) async-start(bf16[8,64,512]{2,1,0:T(8,128)(2,1)} %get-tuple-element.32), calls=%async_computation.1 | async-start | bytes 1048576 | tf_op jit(solution)/shard_map/all_to_all | solution.py:219
  104.4 8.7 %collective-permute-start.25 = (bf16[128,256]{1,0:T(8,128)(2,1)S(1)}, bf16[128,256]{1,0:T(8,128)(2,1)S(1)}, u32[]{:S(2)}, u32[]{:S(2)}) collective-permute-start(bf16[128,256]{1,0:T(8,128)(2,1)S(1)} %get-tuple-element.47), channel_id=1, source_target_pairs={{0,1},{1,2},{2,3},{3,0},{4,5},{5,6},{6,7},{7,4},{8,9},{9,10},{10,1... | collective-permute-start | bytes 196616 | tf_op jit(solution)/shard_map/ppermute | solution.py:223
  104.5 10.4 %collective-permute-start.27 = (bf16[128,256]{1,0:T(8,128)(2,1)S(1)}, bf16[128,256]{1,0:T(8,128)(2,1)S(1)}, u32[]{:S(2)}, u32[]{:S(2)}) collective-permute-start(bf16[128,256]{1,0:T(8,128)(2,1)S(1)} %get-tuple-element.48), channel_id=1, source_target_pairs={{0,3},{1,0},{2,1},{3,2},{4,7},{5,4},{6,5},{7,6},{8,11},{9,8},{10,9... | collective-permute-start | bytes 196616 | tf_op jit(solution)/shard_map/ppermute | solution.py:223
  107.7 7.2 %collective-permute-start.26 = (bf16[128,256]{1,0:T(8,128)(2,1)S(1)}, bf16[128,256]{1,0:T(8,128)(2,1)S(1)}, u32[]{:S(2)}, u32[]{:S(2)}) collective-permute-start(bf16[128,256]{1,0:T(8,128)(2,1)S(1)} %get-tuple-element.49), channel_id=1, source_target_pairs={{0,2},{1,3},{2,0},{3,1},{4,6},{5,7},{6,4},{7,5},{8,10},{9,11},{10,... | collective-permute-start | bytes 196616 | tf_op jit(solution)/shard_map/ppermute | solution.py:223
  109.8 5.9 %collective-permute-start.28 = (bf16[128,256]{1,0:T(8,128)(2,1)S(1)}, bf16[128,256]{1,0:T(8,128)(2,1)S(1)}, u32[]{:S(2)}, u32[]{:S(2)}) collective-permute-start(bf16[128,256]{1,0:T(8,128)(2,1)S(1)} %get-tuple-element.50), channel_id=1, source_target_pairs={{0,4},{4,8},{8,12},{12,0},{1,5},{5,9},{9,13},{13,1},{2,6},{6,10},{... | collective-permute-start | bytes 196616 | tf_op jit(solution)/shard_map/ppermute | solution.py:223
  110.4 5.3 %collective-permute-start.30 = (bf16[128,256]{1,0:T(8,128)(2,1)S(1)}, bf16[128,256]{1,0:T(8,128)(2,1)S(1)}, u32[]{:S(2)}, u32[]{:S(2)}) collective-permute-start(bf16[128,256]{1,0:T(8,128)(2,1)S(1)} %get-tuple-element.51), channel_id=1, source_target_pairs={{0,12},{4,0},{8,4},{12,8},{1,13},{5,1},{9,5},{13,9},{2,14},{6,2},{... | collective-permute-start | bytes 196616 | tf_op jit(solution)/shard_map/ppermute | solution.py:223
  113.1 5.8 %collective-permute-start.29 = (bf16[128,256]{1,0:T(8,128)(2,1)S(1)}, bf16[128,256]{1,0:T(8,128)(2,1)S(1)}, u32[]{:S(2)}, u32[]{:S(2)}) collective-permute-start(bf16[128,256]{1,0:T(8,128)(2,1)S(1)} %get-tuple-element.52), channel_id=1, source_target_pairs={{0,8},{4,12},{8,0},{12,4},{1,9},{5,13},{9,1},{13,5},{2,10},{6,14},... | collective-permute-start | bytes 196616 | tf_op jit(solution)/shard_map/ppermute | solution.py:223
  119.0 5.8 %collective-permute-start.33 = (bf16[64,256]{1,0:T(8,128)(2,1)S(1)}, bf16[64,256]{1,0:T(8,128)(2,1)S(1)}, u32[]{:S(2)}, u32[]{:S(2)}) collective-permute-start(bf16[64,256]{1,0:T(8,128)(2,1)S(1)} %get-tuple-element.60), channel_id=1, source_target_pairs={{0,80},{64,0},{16,64},{80,16},{1,81},{65,1},{17,65},{81,17},{2,82}... | collective-permute-start | bytes 98312 | tf_op jit(solution)/shard_map/ppermute | solution.py:228
  122.3 5.4 %collective-permute-start.32 = (bf16[64,256]{1,0:T(8,128)(2,1)S(1)}, bf16[64,256]{1,0:T(8,128)(2,1)S(1)}, u32[]{:S(2)}, u32[]{:S(2)}) collective-permute-start(bf16[64,256]{1,0:T(8,128)(2,1)S(1)} %get-tuple-element.61), channel_id=1, source_target_pairs={{0,16},{64,80},{16,0},{80,64},{1,17},{65,81},{17,1},{81,65},{2,18}... | collective-permute-start | bytes 98312 | tf_op jit(solution)/shard_map/ppermute | solution.py:228
  123.1 5.1 %collective-permute-start.31 = (bf16[64,256]{1,0:T(8,128)(2,1)S(1)}, bf16[64,256]{1,0:T(8,128)(2,1)S(1)}, u32[]{:S(2)}, u32[]{:S(2)}) collective-permute-start(bf16[64,256]{1,0:T(8,128)(2,1)S(1)} %get-tuple-element.62), channel_id=1, source_target_pairs={{0,64},{64,16},{16,80},{80,0},{1,65},{65,17},{17,81},{81,1},{2,66}... | collective-permute-start | bytes 98312 | tf_op jit(solution)/shard_map/ppermute | solution.py:228
